TPU v7x, 1024 devices: a whole 4x8x16 slice. The times are simulated.
1024 devices in a mesh: space: 128 (over y, z), sample: 8 (over x, core).
Axes of the slice: x: 4, y: 8, z: 16, core: 2. Of those that a mesh axis runs over, the one named last changes fastest.
Arguments:
- features: bfloat16 [8, 128, 1, 8, 8, 768], P('sample', 'space'), may hold values from -12 to 12
- wall_mask: int32 [8, 128, 1, 8, 64], P('sample', 'space'), may hold values 0 or 1
- block_positions: int32 [8, 128, 1], P('sample'), may hold values from -1 to 3, as said below
- dw_kernel: float32 [5, 5, 5, 96], replicated, may hold values from -0.5 to 0.5
- norm_gain: float32 [96], replicated, may hold values from 0.1 to 1.9
- norm_bias: float32 [96], replicated, may hold values from -3 to 3
- w_in: bfloat16 [96, 384], replicated, may hold values from -0.625 to 0.625
- b_in: float32 [384], replicated, may hold values from -3 to 3
- w_out: bfloat16 [384, 96], replicated, may hold values from -0.3125 to 0.3125
- b_out: float32 [96], replicated, may hold values from -3 to 3
- layer_scale: float32 [96], replicated, may hold values from 0.3 to 1.5
- upstream: bfloat16 [8, 128, 1, 8, 8, 768], P('sample', 'space'), may hold values from -6 to 6
Outputs:
- mixed: bfloat16 [8, 128, 1, 8, 8, 768], P('sample', 'space')
- grad_features: bfloat16 [8, 128, 1, 8, 8, 768], P('sample', 'space')
- grad_kernel: float32 [5, 5, 5, 96], replicated
- grad_w_in: float32 [96, 384], replicated
- grad_w_out: float32 [384, 96], replicated
- grad_b_in: float32 [384], replicated
- grad_vectors: float32 [4, 96], replicated
Inputs may be any that keep to these rules, and one draw needn't show every extreme that they name: `block_positions`: in each layer the live slots come first and hold distinct positions; each layer holds exactly 1 block, in slot 0; the first layer of every sample is full and holds position 3.
All inputs are finite; a program needn't handle non-finite values. No bound on the sum of `wall_mask` on one device may be relied on, other than what follows from the above.
Results may differ from a plain program's by a relative error of at most 0.007.
Values may be sent and summed in bfloat16 or wider, within the bound.
A program may use at most 32 MiB of HBM per device.

v0:
```python
import math

import jax
import jax.numpy as jnp
from jax import lax
from jax.sharding import PartitionSpec as P

GRID = 2


GELU_SCALE = 0.7978845608028654
GELU_CUBIC = 0.044715
NORM_EPS = 1e-06


def with_halo(block, sides, width):
    for axis, dim in sides:
        count = lax.axis_size(axis)
        forward = [(i, i + 1) for i in range(count - 1)]
        backward = [(target, source) for source, target in forward]
        low = lax.ppermute(
            lax.slice_in_dim(block, block.shape[dim] - width, None, axis=dim), axis, forward
        )
        high = lax.ppermute(lax.slice_in_dim(block, 0, width, axis=dim), axis, backward)
        block = jnp.concatenate([low, block, high], axis=dim)
    return block


def gelu_value(pre_act):
    inner = GELU_SCALE * (pre_act + GELU_CUBIC * pre_act * pre_act * pre_act)
    return 0.5 * pre_act * (1.0 + jnp.tanh(inner))


def gelu_slope(pre_act):
    inner = GELU_SCALE * (pre_act + GELU_CUBIC * pre_act * pre_act * pre_act)
    tanh_value = jnp.tanh(inner)
    return 0.5 * (1.0 + tanh_value) + 0.5 * pre_act * (
        1.0 - tanh_value * tanh_value
    ) * GELU_SCALE * (1.0 + 3.0 * GELU_CUBIC * pre_act * pre_act)


def expand_fluid(wall_rows, channels):
    block_edge = wall_rows.shape[-2]
    lead_shape = wall_rows.shape[:-2]
    fluid_mask = (
        (1 - wall_rows)
        .astype(jnp.bfloat16)
        .reshape(lead_shape + (block_edge, block_edge, block_edge, 1))
    )
    fluid_mask = jnp.broadcast_to(
        fluid_mask, lead_shape + (block_edge, block_edge, block_edge, channels)
    )
    return fluid_mask.reshape(lead_shape + (block_edge, block_edge, block_edge * channels))


def edge_range(step_now, block_edge):
    if step_now < 0:
        return (block_edge - 2, block_edge)
    if step_now > 0:
        return (0, 2)
    return (0, block_edge)


def select_blocks(source, own_pos, source_pos, step_y, step_x, grid_side):
    own_y = own_pos // grid_side
    own_x = own_pos % grid_side
    target_y = own_y + step_y
    target_x = own_x + step_x
    inside = (
        (own_pos >= 0)
        & (target_y >= 0)
        & (target_y < grid_side)
        & (target_x >= 0)
        & (target_x < grid_side)
    )
    target = target_y * grid_side + target_x
    match = (source_pos[None, :] == target[:, None]) & inside[:, None] & (source_pos[None, :] >= 0)
    chosen = jnp.where(match[:, :, None, None, None], source[None], jnp.zeros((), source.dtype))
    return jnp.sum(chosen, axis=1)


def assemble(own_field, below_rims, above_rims, own_pos, below_pos, above_pos, grid_side):
    block_edge = own_field.shape[1]
    channels = own_field.shape[3] // block_edge
    row_parts = []
    for step_y in (-1, 0, 1):
        col_parts = []
        for step_x in (-1, 0, 1):
            y_low, y_high = edge_range(step_y, block_edge)
            x_low, x_high = edge_range(step_x, block_edge)
            pieces = []
            for source, source_pos in (
                (below_rims, below_pos),
                (own_field, own_pos),
                (above_rims, above_pos),
            ):
                trimmed = source[:, :, y_low:y_high, x_low * channels : x_high * channels]
                pieces.append(
                    select_blocks(trimmed, own_pos, source_pos, step_y, step_x, grid_side)
                )
            col_parts.append(jnp.concatenate(pieces, axis=1))
        row_parts.append(jnp.concatenate(col_parts, axis=3))
    return jnp.concatenate(row_parts, axis=2)


def depthwise(padded, dw_kernel, block_edge):
    channels = dw_kernel.shape[3]
    tap_count = dw_kernel.shape[0]
    running = jnp.zeros(
        (padded.shape[0], block_edge, block_edge, block_edge * channels), jnp.float32
    )
    for tap_z in range(tap_count):
        for tap_y in range(tap_count):
            for tap_x in range(tap_count):
                weight_row = jnp.tile(dw_kernel[tap_z, tap_y, tap_x], block_edge)
                window = padded[
                    :,
                    tap_z : tap_z + block_edge,
                    tap_y : tap_y + block_edge,
                    tap_x * channels : (tap_x + block_edge) * channels,
                ]
                running = running + window.astype(jnp.float32) * weight_row
    return running


def kernel_grad(padded, grad_conv, block_edge, tap_count):
    channels = padded.shape[3] // (block_edge + tap_count - 1)
    grad_wide = grad_conv.astype(jnp.float32)
    rows_list = []
    for tap_z in range(tap_count):
        for tap_y in range(tap_count):
            for tap_x in range(tap_count):
                window = padded[
                    :,
                    tap_z : tap_z + block_edge,
                    tap_y : tap_y + block_edge,
                    tap_x * channels : (tap_x + block_edge) * channels,
                ]
                per_lane = jnp.sum(window.astype(jnp.float32) * grad_wide, axis=(0, 1, 2))
                rows_list.append(jnp.sum(per_lane.reshape(block_edge, channels), axis=0))
    return jnp.stack(rows_list).reshape(tap_count, tap_count, tap_count, channels)


def dense_step(
    conv_slot,
    field_slot,
    live_value,
    upstream_slot,
    norm_gain,
    norm_bias,
    w_in,
    b_in,
    w_out,
    b_out,
    layer_scale,
):
    channels = norm_gain.shape[0]
    slot_shape = field_slot.shape
    conv_rows = conv_slot.reshape(-1, channels)
    row_mean = jnp.mean(conv_rows, axis=1, keepdims=True)
    centred = conv_rows - row_mean
    row_var = jnp.mean(centred * centred, axis=1, keepdims=True)
    inv_std = lax.rsqrt(row_var + NORM_EPS)
    unit_rows = centred * inv_std
    normed = (unit_rows * norm_gain + norm_bias).astype(jnp.bfloat16)
    pre_act = jnp.dot(normed, w_in, preferred_element_type=jnp.float32) + b_in
    activated = gelu_value(pre_act).astype(jnp.bfloat16)
    branch = jnp.dot(activated, w_out, preferred_element_type=jnp.float32) + b_out
    field_rows = field_slot.reshape(-1, channels).astype(jnp.float32)
    mixed = ((field_rows + layer_scale * branch) * live_value).astype(jnp.bfloat16)
    seed_grad = upstream_slot.reshape(-1, channels).astype(jnp.float32) * live_value
    scale_grad = jnp.sum(seed_grad * branch, axis=0)
    grad_branch = (seed_grad * layer_scale).astype(jnp.bfloat16)
    bout_grad = jnp.sum(grad_branch.astype(jnp.float32), axis=0)
    wout_grad = jnp.dot(activated.T, grad_branch, preferred_element_type=jnp.float32)
    grad_act = jnp.dot(grad_branch, w_out.T, preferred_element_type=jnp.float32)
    grad_pre = (grad_act * gelu_slope(pre_act)).astype(jnp.bfloat16)
    bin_grad = jnp.sum(grad_pre.astype(jnp.float32), axis=0)
    win_grad = jnp.dot(normed.T, grad_pre, preferred_element_type=jnp.float32)
    grad_normed = jnp.dot(grad_pre, w_in.T, preferred_element_type=jnp.float32)
    gain_grad = jnp.sum(grad_normed * unit_rows, axis=0)
    bias_grad = jnp.sum(grad_normed, axis=0)
    scaled = grad_normed * norm_gain
    grad_conv = inv_std * (
        scaled
        - jnp.mean(scaled, axis=1, keepdims=True)
        - unit_rows * jnp.mean(scaled * unit_rows, axis=1, keepdims=True)
    )
    grad_conv = grad_conv.astype(jnp.bfloat16).reshape(slot_shape)
    vectors = jnp.stack([gain_grad, bias_grad, bout_grad, scale_grad])
    return (mixed.reshape(slot_shape), grad_conv, (win_grad, wout_grad, bin_grad, vectors))


def local(
    features,
    wall_mask,
    block_positions,
    dw_kernel,
    norm_gain,
    norm_bias,
    w_in,
    b_in,
    w_out,
    b_out,
    layer_scale,
    upstream,
):
    own_field = features[0, 0]
    own_walls = wall_mask[0, 0]
    own_upstream = upstream[0, 0]
    position_table = block_positions[0]
    slot_count = own_field.shape[0]
    block_edge = own_field.shape[1]
    channels = dw_kernel.shape[3]
    tap_count = dw_kernel.shape[0]
    layer_index = lax.axis_index("space")
    layer_count = lax.axis_size("space")
    own_pos = lax.dynamic_index_in_dim(position_table, layer_index, 0, keepdims=False)
    low_row = lax.dynamic_index_in_dim(
        position_table, jnp.maximum(layer_index - 1, 0), 0, keepdims=False
    )
    high_row = lax.dynamic_index_in_dim(
        position_table, jnp.minimum(layer_index + 1, layer_count - 1), 0, keepdims=False
    )
    below_pos = jnp.where(layer_index > 0, low_row, -1)
    above_pos = jnp.where(layer_index < layer_count - 1, high_row, -1)
    live_flag = (own_pos >= 0).astype(jnp.bfloat16)
    fluid_mask = expand_fluid(own_walls, channels)
    masked = own_field * fluid_mask * live_flag[:, None, None, None]
    rims = jnp.concatenate([masked[:, :2], masked[:, block_edge - 2 :]], axis=1)
    extended = with_halo(rims, (("space", 1),), 2)
    padded = assemble(masked, extended[:, :2], extended[:, 6:], own_pos, below_pos, above_pos, GRID)
    conv_out = depthwise(padded, dw_kernel, block_edge)

    def slot_step(slot_items):
        return dense_step(
            slot_items[0],
            slot_items[1],
            slot_items[2],
            slot_items[3],
            norm_gain,
            norm_bias,
            w_in,
            b_in,
            w_out,
            b_out,
            layer_scale,
        )

    mixed, grad_conv, grads = lax.map(
        slot_step, (conv_out, own_field, live_flag.astype(jnp.float32), own_upstream)
    )
    grad_rims = jnp.concatenate([grad_conv[:, :2], grad_conv[:, block_edge - 2 :]], axis=1)
    grad_extended = with_halo(grad_rims, (("space", 1),), 2)
    grad_padded = assemble(
        grad_conv, grad_extended[:, :2], grad_extended[:, 6:], own_pos, below_pos, above_pos, GRID
    )
    back_conv = depthwise(grad_padded, dw_kernel[::-1, ::-1, ::-1], block_edge)
    live_wide = live_flag.astype(jnp.float32)[:, None, None, None]
    seed_grad = own_upstream.astype(jnp.float32) * live_wide
    grad_field = (seed_grad + back_conv * fluid_mask * live_wide).astype(jnp.bfloat16)
    kernel_term = kernel_grad(padded, grad_conv, block_edge, tap_count)
    local_parts = (
        kernel_term,
        jnp.sum(grads[0], axis=0),
        jnp.sum(grads[1], axis=0),
        jnp.sum(grads[2], axis=0),
        jnp.sum(grads[3], axis=0),
    )
    totals = lax.psum(
        (local_parts[0], local_parts[1], local_parts[2], local_parts[3], local_parts[4]),
        ("space", "sample"),
    )
    voxel_total = layer_count * lax.axis_size("sample") * slot_count * block_edge**3
    factor = 1.0 / math.sqrt(voxel_total)
    return (
        mixed[None, None],
        grad_field[None, None],
        totals[0] * factor,
        totals[1] * factor,
        totals[2] * factor,
        totals[3] * factor,
        totals[4] * factor,
    )


def solution(mesh):
    return jax.shard_map(
        local,
        mesh=mesh,
        in_specs=(
            P("sample", "space", None, None, None, None),
            P("sample", "space", None, None, None),
            P("sample", None, None),
            P(),
            P(),
            P(),
            P(),
            P(),
            P(),
            P(),
            P(),
            P("sample", "space", None, None, None, None),
        ),
        out_specs=(
            P("sample", "space", None, None, None, None),
            P("sample", "space", None, None, None, None),
            P(),
            P(),
            P(),
            P(),
            P(),
        ),
        check_vma=False,
    )
```

profile of v0, /device:TPU:1, one launch (start us, length us, event | category | flops | bytes accessed | tf_op | source)
XLA Modules:
  0.0 705.3 jit_solution(16113477991384722591)
XLA Ops:
  7.2 0.6 copy-done.6
  7.9 0.6 constant_dynamic-slice_fusion.2
  13.5 0.7 copy-done.2
  14.3 5.0 collective-permute-start
  19.2 1.3 collective-permute-start.1
  26.2 0.7 copy-done.1
  40.5 13.9 %fusion.129 = f32[1,8,8,768]{3,2,1,0:T(8,128)S(1)} fusion(bf16[1,8,8,768]{3,2,1,0:T(8,128)(2,1)S(1)} %get-tuple-element.199, bf16[1,2,8,768]{3,2,1,0:T(8,128)(2,1)S(1)} %broadcast_select_fusion.7, bf16[1,2,8,768]{3,2,1,0:T(8,128)(2,1)S(1)} %broadcast_select_fusion.9, f32[768]{0:T(1024)S(1)} %mul.3130, f32[768]{0:T(1024)S(1)} %mul.3127, f32[768]{0:T(1024)S(1)} %mul.3124, ...), kind=kLoop, calls=%fused_computation.778 | loop fusion | flops 33718272 | bytes 3025920 | tf_op jit(solution)/shard_map/add | solution.py:122
  54.9 0.6 copy-done.7
  57.2 0.9 fusion.462
  58.1 0.7 convert_reduce_fusion
  58.7 0.9 fusion.458
  62.2 0.7 fusion.235
  62.9 0.9 fusion.236
  63.7 0.9 fusion.250
  64.6 0.8 fusion.251
  65.4 1.0 fusion.252
  66.5 0.9 fusion.253
  67.4 0.8 fusion.254
  68.2 0.8 fusion.238
  69.0 0.9 fusion.239
  69.9 1.1 fusion.237
  83.6 136.5 %all-reduce = (f32[5,5,5,96]{3,2,1,0:T(8,128)S(1)}, f32[384]{0:T(512)S(1)}, f32[4,96]{1,0:T(4,128)S(1)}) all-reduce(f32[5,5,5,96]{3,2,1,0:T(8,128)S(1)} %reshape.2288, f32[384]{0:T(512)S(1)} %get-tuple-element.392, f32[4,96]{1,0:T(4,128)S(1)} %pad_maximum_fusion.26), channel_id=1, replica_groups=mesh['space'=128,'sample'=8] {'space','sample'}, use_global_device_ids=true, to_apply=%region_254.255 | all-reduce | flops 12768 | bytes 102144 | tf_op jit(solution)/shard_map/psum | solution.py:270
  220.1 0.7 broadcast_multiply_fusion.2
  221.4 3.6 collective-permute-start.2
  225.0 0.6 broadcast_multiply_fusion.3
  225.7 0.8 broadcast_in_dim.881
  226.5 1.3 collective-permute-start.3
  227.9 3.2 collective-permute-done.3
  232.6 15.2 %fusion.457 = bf16[1,1,1,8,8,768]{5,4,3,2,1,0:T(8,128)(2,1)} fusion(f32[]{:T(128)S(6)} %squeeze.34, bf16[1,8,8,768]{3,2,1,0:T(8,128)(2,1)S(1)} %broadcast_in_dim.803, f32[768]{0:T(1024)S(1)} %mul.2757, f32[768]{0:T(1024)S(1)} %mul.2760, f32[768]{0:T(1024)S(1)} %mul.2763, f32[768]{0:T(1024)S(1)} %mul.2766, f32[768]{0:T(1024)S(1)} %mul.2769, ...), kind=kLoop, calls=%fused_computation.1144 | loop fusion | flops 34062336 | bytes 3125248 | tf_op jit(solution)/shard_map/broadcast_in_dim | solution.py:278
  247.8 448.4 %all-reduce.4.cloned.1.call-done = (f32[96,384]{1,0:T(8,128)}, f32[384,96]{0,1:T(8,128)}) async-done(((f32[96,384]{1,0:T(8,128)}, f32[384,96]{0,1:T(8,128)}), (f32[96,384]{1,0:T(8,128)}, f32[384,96]{0,1:T(8,128)})) %all-reduce.4.cloned.1.call-update) | async-done | bytes 294928 | tf_op jit(solution)/shard_map/psum | solution.py:270
  696.1 1.6 broadcast_multiply_fusion.1
  697.8 0.7 broadcast_multiply_fusion
  (615 shorter events, 31.5 us)
Async XLA Ops:
  7.2 47.7 %copy-start = (bf16[96,384]{1,0:T(8,128)(2,1)S(1)}, bf16[96,384]{1,0:T(8,128)(2,1)}, u32[]{:S(2)}) copy-start(bf16[96,384]{1,0:T(8,128)(2,1)} %param.18) | copy-start | bytes 221188
  7.2 688.9 %all-reduce.4.cloned.1.call-start = ((), (), s32[]{:S(2)}) async-start(), calls=%async_computation | async-start | bytes 589824 | tf_op jit(solution)/shard_map/psum | solution.py:270
  7.2 0.7 copy-start.6
  11.8 1.3 copy-start.8
  13.3 0.9 copy-start.2
  14.2 6.4 copy-start.5
  14.3 24.6 %collective-permute-start = (bf16[1,2,8,768]{3,2,1,0:T(8,128)(2,1)S(1)}, bf16[1,2,8,768]{3,2,1,0:T(8,128)(2,1)S(1)}, u32[]{:S(2)}, u32[]{:S(2)}) collective-permute-start(bf16[1,2,8,768]{3,2,1,0:T(8,128)(2,1)S(1)} %get-tuple-element.352), channel_id=1, source_target_pairs={{0,8},{8,16},{16,24},{24,32},{32,40},{40,48},{48,56},{56,64},{64,7... | collective-permute-start | bytes 73736 | tf_op jit(solution)/shard_map/ppermute | solution.py:21
  19.2 19.7 %collective-permute-start.1 = (bf16[1,2,8,768]{3,2,1,0:T(8,128)(2,1)S(1)}, bf16[1,2,8,768]{3,2,1,0:T(8,128)(2,1)S(1)}, u32[]{:S(2)}, u32[]{:S(2)}) collective-permute-start(bf16[1,2,8,768]{3,2,1,0:T(8,128)(2,1)S(1)} %get-tuple-element.353), channel_id=1, source_target_pairs={{8,0},{16,8},{24,16},{32,24},{40,32},{48,40},{56,48},{64,56},{72,6... | collective-permute-start | bytes 73736 | tf_op jit(solution)/shard_map/ppermute | solution.py:24
  26.0 0.9 copy-start.1
  54.8 0.7 copy-start.7
  54.9 0.7 copy-start.11
  54.9 0.7 copy-start.12
  55.6 0.9 copy-start.4
  56.1 0.7 copy-start.9
  56.1 0.7 copy-start.10
  221.4 6.5 collective-permute-start.2
  226.5 4.6 collective-permute-start.3
  696.1 1.6 copy-start.3
Sparse Core Ops, SparseCore 0:
  227.9 468.1 all-reduce.3
where the time goes:
time: 708 us; the launch traced here: 705 us
  waiting for transfers between devices  452 us (64%)
  blocking collectives  137 us (19%)
  other arithmetic  48.9 us (7%)
  local copies, waits for them, and re-layouts  26.8 us (4%)
  between operations  26.5 us (4%)
  starting transfers between devices  11.2 us (2%)
    psum x1, waiting for transfers between devices, local(): lax.psum((local_parts[0], local_parts[1], local_parts[2], local_parts[3],...  448 us
    psum x1, blocking collectives, local(): lax.psum((local_parts[0], local_parts[1], local_parts[2], local_parts[3],...  137 us
    broadcast_in_dim x1, other arithmetic, local(): grad_field[None, None]  15.2 us
  transfers between devices with their start and end apart: 5, of which 2 were waited for; matrix products, arithmetic and copies ran while one was open for 4% of the time, Pallas kernels for 0%

commit v1 on v0

v1 whole, which is shorter than its diff:
```python
import math

import jax
import jax.numpy as jnp
from jax import lax
from jax.experimental import pallas as pl
from jax.experimental.pallas import tpu as pltpu
from jax.sharding import PartitionSpec as P

F32 = jnp.float32
BF16 = jnp.bfloat16
MESH = pl.DeviceIdType.MESH

GELU_SCALE = 0.7978845608028654
GELU_CUBIC = 0.044715
NORM_EPS = 1e-06

E = 8
K = 5
C = 96
H = 384
NZ = 16
NY = 8
NS = 8
ROWS = 2
TILE = 16
LANES = 128
W_TILES = 40
K_TILES = 8
W_SHARE = W_TILES // NS
K_SHARE = K_TILES // NS
SHARE = W_SHARE + K_SHARE
PART = -(-SHARE // NY)


def wait_bytes(ref, sem):
    pltpu.make_async_copy(ref, ref, sem).wait()


def send(src, dst, send_sem, recv_sem, device):
    pltpu.make_async_remote_copy(
        src_ref=src,
        dst_ref=dst,
        send_sem=send_sem,
        recv_sem=recv_sem,
        device_id=device,
        device_id_type=MESH,
    ).start()


def send_all(count, me, device, src, dst, send_sem, recv_sem):
    for step in range(1, count):
        peer = lax.rem(me + step, count)
        send(src(peer), dst(step), send_sem, recv_sem, device(peer))


def axis_region(index):
    return jnp.where(index < 2, -1, jnp.where(index < 2 + E, 0, 1))


def shifted(block, tap):
    return pltpu.roll(block, (2 - tap) % E, 1)


def spread_own(dest, column, block, y_index):
    for tap in range(K):
        keep = (axis_region(y_index + tap) == 0).astype(F32)
        dest[tap, column + 2, 2 : 2 + E] = shifted(block, tap) * keep


def clear_sides(dest):
    zeros = jnp.zeros((K, 2, E, E, C), F32)
    dest[:, 0:2, 2 : 2 + E] = zeros
    dest[:, 2 + E : 4 + E, 2 : 2 + E] = zeros


def spread_halo(dest, halo, low, step_y, step_x, exists, y_index):
    for tap in range(K):
        keep_y = (axis_region(y_index + tap) == step_y) & exists
        for region in (-1, 0, 1):
            keep = (keep_y & (step_x == region)).astype(F32)
            first, count = {-1: (0, 2), 0: (2, E), 1: (2 + E, 2)}[region]
            source = (first + E - 2) % E
            block = halo[source : source + count].astype(F32).reshape(count * 2, E, C)
            block = shifted(block, tap).reshape(count, 2, E, C) * keep
            dest[tap, first : first + count, low : low + 2] = block


def conv_planes(field, weights, out, first, last, reverse):
    def plane(index, carry):
        z = lax.rem(index, E)
        total = jnp.zeros((E, E, C), F32)
        for tap_z in range(K):
            for tap_y in range(K):
                window = field[tap_y, :, z + tap_z]
                pair = tap_z * K + tap_y
                for tap_x in range(K):
                    row = weights[K * K - 1 - pair, K - 1 - tap_x] if reverse else weights[pair, tap_x]
                    total = total + window[tap_x : tap_x + E] * row
        out[:, z] = total
        return carry

    lax.fori_loop(first, last, plane, 0)


def body(
    field_ref, wall_ref, pos_ref, dw_ref, gain_ref, bias_ref, win_ref, bin_ref, wout_ref, bout_ref,
    scale_ref, up_ref,
    mixed_ref, gfield_ref, gkernel_ref, gwin_ref, gwout_ref, gbin_ref, gvec_ref,
    weights, padded, gpadded, conv, grad, fluid, field, upstream, mixed,
    normed_all, act_all, gpre_all, gbranch_all, vec_sum, bin_sum, kernel_rows, vec_tile,
    rims, halos, grims, ghalos,
    w_out1, k_out1, w_in1, k_in1, out2, in2, out3, in3, gather4, gather5,
    halo_send, halo_recv, send_sem, recv_sem,
):
    space = lax.axis_index("space")
    sample = lax.axis_index("sample")
    layers = NY * NZ
    chip_y = space // NZ
    chip_z = lax.rem(space, NZ)
    above = (lax.rem(space + 1, layers), sample)
    below = (lax.rem(space + layers - 1, layers), sample)

    def in_sample(peer):
        return (space, peer)

    def in_y(peer):
        return (peer * NZ + chip_z, sample)

    def in_z(peer):
        return (chip_y * NZ + peer, sample)

    barrier = pltpu.get_barrier_semaphore()
    for device in (above, below):
        pl.semaphore_signal(barrier, inc=1, device_id=device, device_id_type=MESH)
    for count, me, device in ((NS, sample, in_sample), (NY, chip_y, in_y), (NZ, chip_z, in_z)):
        for step in range(1, count):
            peer = lax.rem(me + step, count)
            pl.semaphore_signal(barrier, inc=1, device_id=device(peer), device_id_type=MESH)

    y_index = lax.broadcasted_iota(jnp.int32, (E, C), 0)
    lane = lax.broadcasted_iota(jnp.int32, (E, E, E * E), 2)
    sub = lax.broadcasted_iota(jnp.int32, (E, E, E * E), 1)
    walls = jnp.broadcast_to(wall_ref[...].astype(F32)[:, None, :], (E, E, E * E))
    walls = jnp.where(lane // E == sub, walls, 0.0).reshape(E * E, E * E).astype(BF16)
    voxel = lax.broadcasted_iota(jnp.int32, (E * E, C), 0)
    wide = field_ref[...].astype(F32)
    for x in range(E):
        pick = (lax.rem(voxel, E) == x).astype(BF16)
        open_x = 1.0 - jnp.dot(walls, pick, preferred_element_type=F32)
        fluid[x] = open_x.reshape(E, E, C)
        column = wide[:, :, x * C : (x + 1) * C]
        field[x] = column
        masked = column * fluid[x]
        conv[x] = masked
        rims[0, x] = masked[E - 2 :].reshape(2 * E, C).astype(BF16)
        rims[1, x] = masked[:2].reshape(2 * E, C).astype(BF16)

    pl.semaphore_wait(barrier, 2 + NS + NY + NZ - 3)
    send(rims.at[0], halos.at[0], halo_send.at[0], halo_recv.at[0], above)
    send(rims.at[1], halos.at[1], halo_send.at[1], halo_recv.at[1], below)

    wide = up_ref[...].astype(F32)
    for x in range(E):
        upstream[x] = wide[:, :, x * C : (x + 1) * C]
    clear_sides(padded)
    clear_sides(gpadded)

    def own_column(x, carry):
        spread_own(padded, x, conv[x], y_index)
        return carry

    lax.fori_loop(0, E, own_column, 0)

    def spread_weights(pair, carry):
        rows = dw_ref[pair // K, lax.rem(pair, K)]
        weights[pair] = jnp.broadcast_to(rows[:, None, :], (K, E, C))
        return carry

    lax.fori_loop(0, K * K, spread_weights, 0)
    conv_planes(padded, weights, conv, 2, 6, False)

    layer_index = lax.broadcasted_iota(jnp.int32, (1, layers), 1)

    def position(layer):
        return jnp.sum(jnp.where(layer_index == layer, pos_ref[...], 0), axis=1, keepdims=True)

    own_pos, low_pos, high_pos = position(space), position(space - 1), position(space + 1)
    step_low = (low_pos // 2 - own_pos // 2, low_pos % 2 - own_pos % 2)
    step_high = (high_pos // 2 - own_pos // 2, high_pos % 2 - own_pos % 2)

    def place_halos(dest, received):
        spread_halo(dest, received.at[0], 0, *step_low, space > 0, y_index)
        spread_halo(dest, received.at[1], 2 + E, *step_high, space < layers - 1, y_index)

    for side in range(2):
        wait_bytes(halos.at[side], halo_recv.at[side])
    place_halos(padded, halos)
    conv_planes(padded, weights, conv, 6, 10, False)

    vec_sum[...] = jnp.zeros_like(vec_sum)
    bin_sum[...] = jnp.zeros_like(bin_sum)
    gain, bias, bout, scale = gain_ref[...], bias_ref[...], bout_ref[...], scale_ref[...]
    count = ROWS * E * E

    def by_sublane(values):
        return jnp.sum(values.reshape(count // E, E, values.shape[1]), axis=0)

    def dense(step, carry):
        columns = pl.ds(step * ROWS, ROWS)
        rows = pl.ds(pl.multiple_of(step * count, count), count)
        conv_rows = conv[columns].reshape(count, C)
        row_mean = jnp.mean(conv_rows, axis=1, keepdims=True)
        centred = conv_rows - row_mean
        row_var = jnp.mean(centred * centred, axis=1, keepdims=True)
        inv_std = lax.rsqrt(row_var + NORM_EPS)
        unit_rows = centred * inv_std
        normed = (unit_rows * gain + bias).astype(BF16)
        pre_act = jnp.dot(normed, win_ref[...], preferred_element_type=F32) + bin_ref[...]
        square = pre_act * pre_act
        tanh_value = jnp.tanh(GELU_SCALE * (pre_act + GELU_CUBIC * square * pre_act))
        half = 0.5 * (1.0 + tanh_value)
        activated = (pre_act * half).astype(BF16)
        slope = half + 0.5 * pre_act * (1.0 - tanh_value * tanh_value) * (
            GELU_SCALE * (1.0 + 3.0 * GELU_CUBIC * square)
        )
        branch = (
            lax.dot_general(
                activated, wout_ref[...], (((1,), (1,)), ((), ())), preferred_element_type=F32
            )
            + bout
        )
        mixed[columns] = (field[columns].reshape(count, C) + scale * branch).reshape(ROWS, E, E, C)
        seed = upstream[columns].reshape(count, C)
        grad_branch = (seed * scale).astype(BF16)
        grad_act = jnp.dot(grad_branch, wout_ref[...], preferred_element_type=F32)
        grad_pre = (grad_act * slope).astype(BF16)
        grad_normed = lax.dot_general(
            grad_pre, win_ref[...], (((1,), (1,)), ((), ())), preferred_element_type=F32
        )
        scaled = grad_normed * gain
        grad_conv = inv_std * (
            scaled
            - jnp.mean(scaled, axis=1, keepdims=True)
            - unit_rows * jnp.mean(scaled * unit_rows, axis=1, keepdims=True)
        )
        grad[columns] = grad_conv.astype(BF16).astype(F32).reshape(ROWS, E, E, C)
        normed_all[rows] = normed
        act_all[rows] = activated
        gpre_all[rows] = grad_pre
        gbranch_all[rows] = grad_branch
        vec_sum[0] += by_sublane(grad_normed * unit_rows)
        vec_sum[1] += by_sublane(grad_normed)
        vec_sum[2] += by_sublane(grad_branch.astype(F32))
        vec_sum[3] += by_sublane(seed * branch)
        bin_sum[...] += by_sublane(grad_pre.astype(F32))
        return carry

    lax.fori_loop(0, E // ROWS, dense, 0)

    def grad_rims(x, carry):
        grims[0, x] = grad[x, E - 2 :].reshape(2 * E, C).astype(BF16)
        grims[1, x] = grad[x, :2].reshape(2 * E, C).astype(BF16)
        return carry

    lax.fori_loop(0, E, grad_rims, 0)
    send(grims.at[0], ghalos.at[0], halo_send.at[2], halo_recv.at[2], above)
    send(grims.at[1], ghalos.at[1], halo_send.at[3], halo_recv.at[3], below)

    by_rows = (((0,), (0,)), ((), ()))
    for base, left, right in ((0, normed_all, gpre_all), (18, gbranch_all, act_all)):
        product = lax.dot_general(left[...], right[...], by_rows, preferred_element_type=F32)
        for part in range(H // LANES):
            piece = product[:, part * LANES : (part + 1) * LANES].astype(BF16)
            w_out1[base + 6 * part : base + 6 * part + 6] = piece.reshape(6, TILE, LANES)
    vec_tile[...] = jnp.zeros_like(vec_tile)
    bin_row = jnp.sum(bin_sum[...], axis=0, keepdims=True)
    for part in range(H // LANES):
        vec_tile[part : part + 1] = bin_row[:, part * LANES : (part + 1) * LANES]
    for row in range(4):
        vec_tile[3 + row : 4 + row, 0:C] = jnp.sum(vec_sum[row], axis=0, keepdims=True)
    w_out1[36] = vec_tile[...].astype(BF16)
    w_out1[37:W_TILES] = jnp.zeros((W_TILES - 37, TILE, LANES), BF16)
    send_all(
        NS, sample, in_sample, lambda peer: w_out1.at[pl.ds(peer * W_SHARE, W_SHARE)],
        lambda step: w_in1.at[step - 1], send_sem.at[0], recv_sem.at[0],
    )

    kernel_rows[...] = jnp.zeros_like(kernel_rows)

    def kernel_pair(pair, carry):
        tap_z = pair // K
        tap_y = lax.rem(pair, K)
        sums = [jnp.zeros((E, C), F32) for _ in range(K)]
        for z in range(E):
            window = padded[tap_y, :, z + tap_z]
            factor = grad[:, z]
            for tap_x in range(K):
                sums[tap_x] = sums[tap_x] + jnp.sum(window[tap_x : tap_x + E] * factor, axis=0)
        for tap_x in range(K):
            total = jnp.sum(sums[tap_x], axis=0, keepdims=True)
            kernel_rows[pl.ds(pair * K + tap_x, 1), 0:C] = total
        return carry

    lax.fori_loop(0, K * K, kernel_pair, 0)
    k_out1[...] = kernel_rows[...].astype(BF16).reshape(K_TILES, TILE, LANES)
    send_all(
        NS, sample, in_sample, lambda peer: k_out1.at[pl.ds(peer * K_SHARE, K_SHARE)],
        lambda step: k_in1.at[step - 1], send_sem.at[1], recv_sem.at[1],
    )

    def own_grad_column(x, carry):
        spread_own(gpadded, x, grad[x], y_index)
        return carry

    lax.fori_loop(0, E, own_grad_column, 0)
    conv_planes(gpadded, weights, conv, 2, 6, True)

    wait_bytes(w_in1, recv_sem.at[0])
    wait_bytes(k_in1, recv_sem.at[1])
    w_total = w_out1[pl.ds(sample * W_SHARE, W_SHARE)].astype(F32)
    k_total = k_out1[pl.ds(sample * K_SHARE, K_SHARE)].astype(F32)
    for step in range(NS - 1):
        w_total = w_total + w_in1[step].astype(F32)
        k_total = k_total + k_in1[step].astype(F32)
    out2[0:W_SHARE] = w_total.astype(BF16)
    out2[W_SHARE:SHARE] = k_total.astype(BF16)
    if NY * PART > SHARE:
        out2[SHARE : NY * PART] = jnp.zeros((NY * PART - SHARE, TILE, LANES), BF16)
    send_all(
        NY, chip_y, in_y, lambda peer: out2.at[pl.ds(peer * PART, PART)],
        lambda step: in2.at[step - 1], send_sem.at[2], recv_sem.at[2],
    )

    for side in range(2):
        wait_bytes(ghalos.at[side], halo_recv.at[2 + side])
    place_halos(gpadded, ghalos)
    conv_planes(gpadded, weights, conv, 6, 10, True)

    wait_bytes(in2, recv_sem.at[2])
    total = out2[pl.ds(chip_y * PART, PART)].astype(F32)
    for step in range(NY - 1):
        total = total + in2[step].astype(F32)
    out3[...] = total.astype(BF16)
    send_all(
        NZ, chip_z, in_z, lambda peer: out3,
        lambda step: in3.at[step - 1], send_sem.at[3], recv_sem.at[3],
    )

    for x in range(E):
        lanes = slice(x * C, (x + 1) * C)
        mixed_ref[:, :, lanes] = mixed[x].astype(BF16)
        gfield_ref[:, :, lanes] = (upstream[x] + conv[x] * fluid[x]).astype(BF16)

    wait_bytes(in3, recv_sem.at[3])
    total = out3[...].astype(F32)
    for step in range(NZ - 1):
        total = total + in3[step].astype(F32)
    mine = pl.ds(chip_y * PART, PART)
    gather4[mine] = total.astype(BF16)
    send_all(
        NY, chip_y, in_y, lambda peer: gather4.at[mine],
        lambda step: gather4.at[mine], send_sem.at[4], recv_sem.at[4],
    )
    wait_bytes(gather4.at[0 : (NY - 1) * PART], recv_sem.at[4])
    gather5[sample] = gather4[0:SHARE]
    send_all(
        NS, sample, in_sample, lambda peer: gather5.at[sample],
        lambda step: gather5.at[sample], send_sem.at[5], recv_sem.at[5],
    )
    wait_bytes(gather5.at[0 : NS - 1], recv_sem.at[5])

    factor = 1.0 / math.sqrt(NS * layers * E**3)

    def tile_of(index):
        return gather5[index // W_SHARE, index % W_SHARE].astype(F32) * factor

    for part in range(H // LANES):
        lanes = slice(part * LANES, (part + 1) * LANES)
        for row in range(6):
            gwin_ref[row * TILE : (row + 1) * TILE, lanes] = tile_of(6 * part + row)
            gwout_ref[row * TILE : (row + 1) * TILE, lanes] = tile_of(18 + 6 * part + row)
    last = tile_of(36)
    for part in range(H // LANES):
        gbin_ref[0:1, part * LANES : (part + 1) * LANES] = last[part : part + 1]
    gvec_ref[...] = last[3:7, 0:C]
    rows = gather5[:, W_SHARE:SHARE].astype(F32).reshape(K_TILES * TILE, LANES)[:, 0:C] * factor
    for pair in range(K * K):
        gkernel_ref[pair // K, pair % K] = rows[pair * K : (pair + 1) * K]

    for side in range(2):
        wait_bytes(rims.at[side], halo_send.at[side])
        wait_bytes(grims.at[side], halo_send.at[2 + side])
    for index, ref in enumerate((w_in1, k_in1, in2, in3, gather4.at[0 : (NY - 1) * PART], gather5.at[0 : NS - 1])):
        wait_bytes(ref, send_sem.at[index])


def local(
    features, wall_mask, block_positions, dw_kernel, norm_gain, norm_bias, w_in, b_in, w_out, b_out,
    layer_scale, upstream,
):
    voxels = (E, E, E, C)
    spread = (K, E + 4, E + 4, E, C)
    rows = E**3
    vmem = pl.BlockSpec(memory_space=pltpu.VMEM)
    outs = (
        jax.ShapeDtypeStruct((E, E, E * C), BF16),
        jax.ShapeDtypeStruct((E, E, E * C), BF16),
        jax.ShapeDtypeStruct((K, K, K, C), F32),
        jax.ShapeDtypeStruct((C, H), F32),
        jax.ShapeDtypeStruct((C, H), F32),
        jax.ShapeDtypeStruct((1, H), F32),
        jax.ShapeDtypeStruct((4, C), F32),
    )
    scratch = [
        pltpu.VMEM((K * K, K, E, C), F32),
        pltpu.VMEM(spread, F32),
        pltpu.VMEM(spread, F32),
        pltpu.VMEM(voxels, F32),
        pltpu.VMEM(voxels, F32),
        pltpu.VMEM(voxels, F32),
        pltpu.VMEM(voxels, F32),
        pltpu.VMEM(voxels, F32),
        pltpu.VMEM(voxels, F32),
        pltpu.VMEM((rows, C), BF16),
        pltpu.VMEM((rows, H), BF16),
        pltpu.VMEM((rows, H), BF16),
        pltpu.VMEM((rows, C), BF16),
        pltpu.VMEM((4, E, C), F32),
        pltpu.VMEM((E, H), F32),
        pltpu.VMEM((K_TILES * TILE, LANES), F32),
        pltpu.VMEM((TILE, LANES), F32),
        pltpu.VMEM((2, E, 2 * E, C), BF16),
        pltpu.VMEM((2, E, 2 * E, C), BF16),
        pltpu.VMEM((2, E, 2 * E, C), BF16),
        pltpu.VMEM((2, E, 2 * E, C), BF16),
        pltpu.VMEM((W_TILES, TILE, LANES), BF16),
        pltpu.VMEM((K_TILES, TILE, LANES), BF16),
        pltpu.VMEM((NS - 1, W_SHARE, TILE, LANES), BF16),
        pltpu.VMEM((NS - 1, K_SHARE, TILE, LANES), BF16),
        pltpu.VMEM((NY * PART, TILE, LANES), BF16),
        pltpu.VMEM((NY - 1, PART, TILE, LANES), BF16),
        pltpu.VMEM((PART, TILE, LANES), BF16),
        pltpu.VMEM((NZ - 1, PART, TILE, LANES), BF16),
        pltpu.VMEM((NY * PART, TILE, LANES), BF16),
        pltpu.VMEM((NS, SHARE, TILE, LANES), BF16),
        pltpu.SemaphoreType.DMA((4,)),
        pltpu.SemaphoreType.DMA((4,)),
        pltpu.SemaphoreType.DMA((6,)),
        pltpu.SemaphoreType.DMA((6,)),
    ]
    results = pl.pallas_call(
        body,
        out_shape=outs,
        in_specs=[vmem] * 12,
        out_specs=[vmem] * 7,
        scratch_shapes=scratch,
        compiler_params=pltpu.CompilerParams(
            collective_id=0, has_side_effects=True, vmem_limit_bytes=48 * 1024 * 1024
        ),
        cost_estimate=pl.CostEstimate(flops=400_000_000, bytes_accessed=1_500_000, transcendentals=200_000),
        name="block_step",
    )(
        features[0, 0, 0],
        wall_mask[0, 0, 0],
        block_positions[:, :, 0],
        dw_kernel,
        norm_gain[None],
        norm_bias[None],
        w_in,
        b_in[None],
        w_out.T,
        b_out[None],
        layer_scale[None],
        upstream[0, 0, 0],
    )
    mixed, gfield, gkernel, gwin, gwout, gbin, gvec = results
    return (mixed[None, None, None], gfield[None, None, None], gkernel, gwin, gwout.T, gbin[0], gvec)


def solution(mesh):
    sharded = P("sample", "space", None, None, None, None)
    return jax.shard_map(
        local,
        mesh=mesh,
        in_specs=(
            sharded,
            P("sample", "space", None, None, None),
            P("sample", None, None),
            P(), P(), P(), P(), P(), P(), P(), P(),
            sharded,
        ),
        out_specs=(sharded, sharded, P(), P(), P(), P(), P()),
        check_vma=False,
    )
```

time: 708 us -> 73.9 us (0.10)
  waiting for transfers between devices: 452 us -> 0 us
  blocking collectives: 137 us -> 0 us
  Pallas kernels: 0 us -> 62.6 us
  other arithmetic: 48.9 us -> 0.6 us
  between operations: 26.5 us -> 0.68 us
  local copies, waits for them, and re-layouts: 26.8 us -> 9.66 us
  starting transfers between devices: 11.2 us -> 0 us
    psum x1 -> x0, waiting for transfers between devices: 448 us -> none  [local(): lax.psum((local_parts[0], local_parts[1], local_parts[2], local_parts[3],...]
    psum x1 -> x0, blocking collectives: 137 us -> none  [local(): lax.psum((local_parts[0], local_parts[1], local_parts[2], local_parts[3],...]
    pallas_call x0 -> x1, Pallas kernels: none -> 62.6 us  [local(): pl.pallas_call(body, out_shape=outs, in_specs=[vmem] * 12, out_specs=[vme...]
    broadcast_in_dim x1 -> x0, other arithmetic: 15.2 us -> none  [local(): grad_field[None, None]]
    add x1 -> x0, other arithmetic: 13.9 us -> none  [depthwise(): running = running + window.astype(jnp.float32) * weight_row]
    reduce_sum x142 -> x0, other arithmetic: 13.4 us -> none  [the longest x15 10.4 us: kernel_grad(): per_lane = jnp.sum(window.astype(jnp.float32) * grad_wide, axis=(0, 1, 2))]
    ppermute x4 -> x0, starting transfers between devices: 11.2 us -> none  [the longest x2 8.6 us: with_halo(): lax.ppermute(lax.slice_in_dim(block, block.shape[dim] - width, None, axis...]
    mul x127 -> x0, local copies, waits for them, and re-layouts: 9.72 us -> none  [the longest x125 9.46 us: depthwise(): running = running + window.astype(jnp.float32) * weight_row]
  transfers between devices with their start and end apart: 5 -> 0, of which waited for: 2 -> 0; matrix products, arithmetic and copies ran while one was open for 4% -> 0% of each run, Pallas kernels for 0% -> 0%
where the time goes in v1:
time: 73.9 us; the launch traced here: 73.5 us
  Pallas kernels  62.6 us (85%)
  local copies, waits for them, and re-layouts  9.66 us (13%)
    pallas_call x1, Pallas kernels, local(): pl.pallas_call(body, out_shape=outs, in_specs=[vmem] * 12, out_specs=[vme...  62.6 us
    unnamed x28, local copies, waits for them, and re-layouts  8.97 us

profile of v1, /device:TPU:1, one launch (start us, length us, event | category | flops | bytes accessed | tf_op | source)
XLA Modules:
  0.0 73.5 jit_solution(16010755058665339475)
XLA Ops:
  0.6 0.7 broadcast_in_dim.23.bin_ref
  1.3 0.0 copy-start.5
  1.3 0.0 copy-start.9
  1.3 0.0 copy-start.10
  1.3 0.0 copy-start.6
  1.3 0.0 copy-start.7
  1.3 0.0 copy-start.8
  1.4 0.6 copy-done.5
  2.0 0.0 copy-done.9
  2.0 0.0 copy-done.10
  2.0 0.0 copy-done.6
  2.0 0.0 copy-done.7
  2.0 0.0 copy-done.8
  2.1 0.0 copy-start
  2.1 0.9 %copy-done = f32[5,5,5,96]{3,2,1,0:T(8,128)S(1)} copy-done((f32[5,5,5,96]{3,2,1,0:T(8,128)S(1)}, f32[5,5,5,96]{3,2,1,0:T(8,128)}, u32[]{:S(2)}) %copy-start) | copy-done | bytes 48024
  2.9 0.0 copy-start.1
  2.9 0.9 %copy-done.1 = bf16[1,1,1,8,8,768]{5,4,3,2,1,0:T(8,128)(2,1)S(1)} copy-done((bf16[1,1,1,8,8,768]{5,4,3,2,1,0:T(8,128)(2,1)S(1)}, bf16[1,1,1,8,8,768]{5,4,3,2,1,0:T(8,128)(2,1)}, u32[]{:S(2)}) %copy-start.1) | copy-done | bytes 98328
  3.8 0.0 copy-start.2
  3.8 0.9 %copy-done.2 = bf16[1,1,1,8,8,768]{5,4,3,2,1,0:T(8,128)(2,1)S(1)} copy-done((bf16[1,1,1,8,8,768]{5,4,3,2,1,0:T(8,128)(2,1)S(1)}, bf16[1,1,1,8,8,768]{5,4,3,2,1,0:T(8,128)(2,1)}, u32[]{:S(2)}) %copy-start.2) | copy-done | bytes 98328
  4.7 0.0 copy-start.3
  4.7 0.9 %copy-done.3 = bf16[96,384]{1,0:T(8,128)(2,1)S(1)} copy-done((bf16[96,384]{1,0:T(8,128)(2,1)S(1)}, bf16[96,384]{1,0:T(8,128)(2,1)}, u32[]{:S(2)}) %copy-start.3) | copy-done | bytes 73752
  5.6 0.0 copy-start.4
  5.6 0.9 %copy-done.4 = bf16[384,96]{0,1:T(8,128)(2,1)S(1)} copy-done((bf16[384,96]{0,1:T(8,128)(2,1)S(1)}, bf16[384,96]{0,1:T(8,128)(2,1)}, u32[]{:S(2)}) %copy-start.4) | copy-done | bytes 73752
  6.5 62.6 %block_step.1 = (bf16[8,8,768]{2,1,0:T(8,128)(2,1)S(1)}, bf16[8,8,768]{2,1,0:T(8,128)(2,1)S(1)}, f32[5,5,5,96]{3,2,1,0:T(8,128)S(1)}, f32[96,384]{1,0:T(8,128)S(...) custom-call(bf16[8,8,768]{2,1,0:T(8,128)(2,1)S(1)} %bitcast.15, s32[8,64]{1,0:T(8,128)S(1)} %bitcast.18, ...), custom_call_target="tpu_custom_call" | custom-call | flops 400000000 | bytes 1500000 | tf_op jit(solution)/shard_map/block_step/pallas_call | solution.py:452
  69.1 0.6 reduce
  69.7 0.6 copy.25
  70.3 0.6 copy.26
  71.0 0.6 copy.27
  71.6 0.7 copy.28
  72.3 0.7 copy.29
  72.9 0.6 copy.30
Async XLA Ops:
  1.3 0.7 copy-start.5
  1.3 0.7 copy-start.9
  1.3 0.7 copy-start.10
  1.3 0.7 copy-start.6
  1.3 0.7 copy-start.7
  1.3 0.7 copy-start.8
  2.1 0.9 %copy-start = (f32[5,5,5,96]{3,2,1,0:T(8,128)S(1)}, f32[5,5,5,96]{3,2,1,0:T(8,128)}, u32[]{:S(2)}) copy-start(f32[5,5,5,96]{3,2,1,0:T(8,128)} %dw_ref.1) | copy-start | bytes 144004
  2.9 0.9 %copy-start.1 = (bf16[1,1,1,8,8,768]{5,4,3,2,1,0:T(8,128)(2,1)S(1)}, bf16[1,1,1,8,8,768]{5,4,3,2,1,0:T(8,128)(2,1)}, u32[]{:S(2)}) copy-start(bf16[1,1,1,8,8,768]{5,4,3,2,1,0:T(8,128)(2,1)} %param.12) | copy-start | bytes 294916
  3.8 0.9 %copy-start.2 = (bf16[1,1,1,8,8,768]{5,4,3,2,1,0:T(8,128)(2,1)S(1)}, bf16[1,1,1,8,8,768]{5,4,3,2,1,0:T(8,128)(2,1)}, u32[]{:S(2)}) copy-start(bf16[1,1,1,8,8,768]{5,4,3,2,1,0:T(8,128)(2,1)} %param.23) | copy-start | bytes 294916
  4.7 0.9 %copy-start.3 = (bf16[96,384]{1,0:T(8,128)(2,1)S(1)}, bf16[96,384]{1,0:T(8,128)(2,1)}, u32[]{:S(2)}) copy-start(bf16[96,384]{1,0:T(8,128)(2,1)} %win_ref.1) | copy-start | bytes 221188
  5.6 0.9 %copy-start.4 = (bf16[384,96]{0,1:T(8,128)(2,1)S(1)}, bf16[384,96]{0,1:T(8,128)(2,1)}, u32[]{:S(2)}) copy-start(bf16[384,96]{0,1:T(8,128)(2,1)} %param.20) | copy-start | bytes 221188

commit v2 on v1

--- a/solution.py
+++ b/solution.py
@@ -15,6 +15,7 @@
 GELU_CUBIC = 0.044715
 NORM_EPS = 1e-06
 
+VMEM_BYTES = 62 * 1024 * 1024
 E = 8
 K = 5
 C = 96
@@ -29,8 +30,7 @@
 K_TILES = 8
 W_SHARE = W_TILES // NS
 K_SHARE = K_TILES // NS
-SHARE = W_SHARE + K_SHARE
-PART = -(-SHARE // NY)
+PART = -(-W_SHARE // NY)
 
 
 def wait_bytes(ref, sem):
@@ -48,10 +48,26 @@
     ).start()
 
 
-def send_all(count, me, device, src, dst, send_sem, recv_sem):
-    for step in range(1, count):
-        peer = lax.rem(me + step, count)
-        send(src(peer), dst(step), send_sem, recv_sem, device(peer))
+def ring_order(count):
+    return sorted(range(1, count), key=lambda step: -min(step, count - step))
+
+
+def sample_order():
+    chips = NS // 2
+    steps = [(x, core) for x in range(chips) for core in range(2) if (x, core) != (0, 0)]
+    return sorted(steps, key=lambda step: -min(step[0], chips - step[0]))
+
+
+def send_all(peers, src, dst, send_sem, recv_sem):
+    for slot, (index, device) in enumerate(peers):
+        send(src(index), dst(slot), send_sem, recv_sem, device)
+
+
+def add_all(total, parts, count):
+    total = total.astype(F32)
+    for slot in range(count):
+        total = total + parts[slot].astype(F32)
+    return total
 
 
 def axis_region(index):
@@ -104,15 +120,36 @@
 
 
 def body(
+    field_hbm, wall_hbm, pos_hbm, dw_hbm, gain_hbm, bias_hbm, win_hbm, bin_hbm, wout_hbm, bout_hbm,
+    scale_hbm, up_hbm,
+    mixed_hbm, gfield_hbm, gkernel_hbm, gwin_hbm, gwout_hbm, gbin_hbm, gvec_hbm,
+    weights, padded, gpadded, conv, grad, fluid, field, upstream, mixed,
+    normed_all, act_all, gpre_all, gbranch_all, vec_sum, bin_sum, kernel_rows, vec_tile,
+    rims, halos, grims, ghalos,
+    w_out1, w_in1, w_out2, w_in2, w_out3, w_in3, w_share, w_all,
+    k_out1, k_in1, k_out2, k_in2, k_out3, k_in3, k_all,
     field_ref, wall_ref, pos_ref, dw_ref, gain_ref, bias_ref, win_ref, bin_ref, wout_ref, bout_ref,
     scale_ref, up_ref,
     mixed_ref, gfield_ref, gkernel_ref, gwin_ref, gwout_ref, gbin_ref, gvec_ref,
-    weights, padded, gpadded, conv, grad, fluid, field, upstream, mixed,
-    normed_all, act_all, gpre_all, gbranch_all, vec_sum, bin_sum, kernel_rows, vec_tile,
-    rims, halos, grims, ghalos,
-    w_out1, k_out1, w_in1, k_in1, out2, in2, out3, in3, gather4, gather5,
-    halo_send, halo_recv, send_sem, recv_sem,
+    halo_send, halo_recv, send_sem, recv_sem, load_sem, store_sem,
 ):
+    stores = [
+        pltpu.make_async_copy(source, dest, store_sem.at[index])
+        for index, (source, dest) in enumerate((
+            (mixed_ref, mixed_hbm), (gfield_ref, gfield_hbm), (gkernel_ref, gkernel_hbm),
+            (gwin_ref, gwin_hbm), (gwout_ref, gwout_hbm), (gbin_ref, gbin_hbm), (gvec_ref, gvec_hbm),
+        ))
+    ]
+    loads = [
+        pltpu.make_async_copy(source, dest, load_sem.at[index])
+        for index, (source, dest) in enumerate((
+            (field_hbm, field_ref), (wall_hbm, wall_ref), (dw_hbm, dw_ref), (up_hbm, up_ref),
+            (pos_hbm, pos_ref), (gain_hbm, gain_ref), (bias_hbm, bias_ref), (win_hbm, win_ref),
+            (bin_hbm, bin_ref), (wout_hbm, wout_ref), (bout_hbm, bout_ref), (scale_hbm, scale_ref),
+        ))
+    ]
+    for load in loads:
+        load.start()
     space = lax.axis_index("space")
     sample = lax.axis_index("sample")
     layers = NY * NZ
@@ -121,23 +158,27 @@
     above = (lax.rem(space + 1, layers), sample)
     below = (lax.rem(space + layers - 1, layers), sample)
 
-    def in_sample(peer):
-        return (space, peer)
-
-    def in_y(peer):
-        return (peer * NZ + chip_z, sample)
-
-    def in_z(peer):
-        return (chip_y * NZ + peer, sample)
+    x_peers = []
+    for step_x, step_core in sample_order():
+        x = lax.rem(sample // 2 + step_x, NS // 2)
+        index = x * 2 + lax.rem(sample + step_core, 2)
+        x_peers.append((index, (space, index)))
+    y_peers = []
+    for step in ring_order(NY):
+        index = lax.rem(chip_y + step, NY)
+        y_peers.append((index, (index * NZ + chip_z, sample)))
+    z_peers = []
+    for step in ring_order(NZ):
+        index = lax.rem(chip_z + step, NZ)
+        z_peers.append((index, (chip_y * NZ + index, sample)))
 
     barrier = pltpu.get_barrier_semaphore()
-    for device in (above, below):
+    partners = [above, below] + [device for _, device in x_peers + y_peers + z_peers]
+    for device in partners:
         pl.semaphore_signal(barrier, inc=1, device_id=device, device_id_type=MESH)
-    for count, me, device in ((NS, sample, in_sample), (NY, chip_y, in_y), (NZ, chip_z, in_z)):
-        for step in range(1, count):
-            peer = lax.rem(me + step, count)
-            pl.semaphore_signal(barrier, inc=1, device_id=device(peer), device_id_type=MESH)
-
+
+    loads[0].wait()
+    loads[1].wait()
     y_index = lax.broadcasted_iota(jnp.int32, (E, C), 0)
     lane = lax.broadcasted_iota(jnp.int32, (E, E, E * E), 2)
     sub = lax.broadcasted_iota(jnp.int32, (E, E, E * E), 1)
@@ -156,10 +197,12 @@
         rims[0, x] = masked[E - 2 :].reshape(2 * E, C).astype(BF16)
         rims[1, x] = masked[:2].reshape(2 * E, C).astype(BF16)
 
-    pl.semaphore_wait(barrier, 2 + NS + NY + NZ - 3)
+    pl.semaphore_wait(barrier, len(partners))
     send(rims.at[0], halos.at[0], halo_send.at[0], halo_recv.at[0], above)
     send(rims.at[1], halos.at[1], halo_send.at[1], halo_recv.at[1], below)
 
+    for load in loads[2:]:
+        load.wait()
     wide = up_ref[...].astype(F32)
     for x in range(E):
         upstream[x] = wide[:, :, x * C : (x + 1) * C]
@@ -200,6 +243,7 @@
 
     vec_sum[...] = jnp.zeros_like(vec_sum)
     bin_sum[...] = jnp.zeros_like(bin_sum)
+    b_in = jnp.concatenate([bin_ref[part : part + 1] for part in range(H // LANES)], axis=1)
     gain, bias, bout, scale = gain_ref[...], bias_ref[...], bout_ref[...], scale_ref[...]
     count = ROWS * E * E
 
@@ -216,7 +260,7 @@
         inv_std = lax.rsqrt(row_var + NORM_EPS)
         unit_rows = centred * inv_std
         normed = (unit_rows * gain + bias).astype(BF16)
-        pre_act = jnp.dot(normed, win_ref[...], preferred_element_type=F32) + bin_ref[...]
+        pre_act = jnp.dot(normed, win_ref[...], preferred_element_type=F32) + b_in
         square = pre_act * pre_act
         tanh_value = jnp.tanh(GELU_SCALE * (pre_act + GELU_CUBIC * square * pre_act))
         half = 0.5 * (1.0 + tanh_value)
@@ -282,8 +326,8 @@
     w_out1[36] = vec_tile[...].astype(BF16)
     w_out1[37:W_TILES] = jnp.zeros((W_TILES - 37, TILE, LANES), BF16)
     send_all(
-        NS, sample, in_sample, lambda peer: w_out1.at[pl.ds(peer * W_SHARE, W_SHARE)],
-        lambda step: w_in1.at[step - 1], send_sem.at[0], recv_sem.at[0],
+        x_peers, lambda peer: w_out1.at[pl.ds(peer * W_SHARE, W_SHARE)],
+        lambda slot: w_in1.at[slot], send_sem.at[0], recv_sem.at[0],
     )
 
     kernel_rows[...] = jnp.zeros_like(kernel_rows)
@@ -305,8 +349,8 @@
     lax.fori_loop(0, K * K, kernel_pair, 0)
     k_out1[...] = kernel_rows[...].astype(BF16).reshape(K_TILES, TILE, LANES)
     send_all(
-        NS, sample, in_sample, lambda peer: k_out1.at[pl.ds(peer * K_SHARE, K_SHARE)],
-        lambda step: k_in1.at[step - 1], send_sem.at[1], recv_sem.at[1],
+        x_peers, lambda peer: k_out1.at[pl.ds(peer * K_SHARE, K_SHARE)],
+        lambda slot: k_in1.at[slot], send_sem.at[5], recv_sem.at[5],
     )
 
     def own_grad_column(x, carry):
@@ -314,66 +358,86 @@
         return carry
 
     lax.fori_loop(0, E, own_grad_column, 0)
+
+    wait_bytes(w_in1, recv_sem.at[0])
+    total = add_all(w_out1[pl.ds(sample * W_SHARE, W_SHARE)], w_in1, NS - 1)
+    w_out2[0:W_SHARE] = total.astype(BF16)
+    if NY * PART > W_SHARE:
+        w_out2[W_SHARE : NY * PART] = jnp.zeros((NY * PART - W_SHARE, TILE, LANES), BF16)
+    send_all(
+        y_peers, lambda peer: w_out2.at[pl.ds(peer * PART, PART)],
+        lambda slot: w_in2.at[slot], send_sem.at[1], recv_sem.at[1],
+    )
+
     conv_planes(gpadded, weights, conv, 2, 6, True)
 
-    wait_bytes(w_in1, recv_sem.at[0])
-    wait_bytes(k_in1, recv_sem.at[1])
-    w_total = w_out1[pl.ds(sample * W_SHARE, W_SHARE)].astype(F32)
-    k_total = k_out1[pl.ds(sample * K_SHARE, K_SHARE)].astype(F32)
-    for step in range(NS - 1):
-        w_total = w_total + w_in1[step].astype(F32)
-        k_total = k_total + k_in1[step].astype(F32)
-    out2[0:W_SHARE] = w_total.astype(BF16)
-    out2[W_SHARE:SHARE] = k_total.astype(BF16)
-    if NY * PART > SHARE:
-        out2[SHARE : NY * PART] = jnp.zeros((NY * PART - SHARE, TILE, LANES), BF16)
-    send_all(
-        NY, chip_y, in_y, lambda peer: out2.at[pl.ds(peer * PART, PART)],
-        lambda step: in2.at[step - 1], send_sem.at[2], recv_sem.at[2],
+    wait_bytes(k_in1, recv_sem.at[5])
+    total = add_all(k_out1[pl.ds(sample * K_SHARE, K_SHARE)], k_in1, NS - 1)
+    k_out2[...] = total.astype(BF16)
+    send_all(
+        y_peers, lambda peer: k_out2, lambda slot: k_in2.at[slot], send_sem.at[6], recv_sem.at[6]
+    )
+
+    wait_bytes(w_in2, recv_sem.at[1])
+    total = add_all(w_out2[pl.ds(chip_y * PART, PART)], w_in2, NY - 1)
+    w_out3[...] = total.astype(BF16)
+    send_all(
+        z_peers, lambda peer: w_out3, lambda slot: w_in3.at[slot], send_sem.at[2], recv_sem.at[2]
     )
 
     for side in range(2):
         wait_bytes(ghalos.at[side], halo_recv.at[2 + side])
     place_halos(gpadded, ghalos)
+
+    wait_bytes(k_in2, recv_sem.at[6])
+    k_out3[...] = add_all(k_out2[...], k_in2, NY - 1).astype(BF16)
+    send_all(
+        z_peers, lambda peer: k_out3, lambda slot: k_in3.at[slot], send_sem.at[7], recv_sem.at[7]
+    )
+
     conv_planes(gpadded, weights, conv, 6, 10, True)
-
-    wait_bytes(in2, recv_sem.at[2])
-    total = out2[pl.ds(chip_y * PART, PART)].astype(F32)
-    for step in range(NY - 1):
-        total = total + in2[step].astype(F32)
-    out3[...] = total.astype(BF16)
-    send_all(
-        NZ, chip_z, in_z, lambda peer: out3,
-        lambda step: in3.at[step - 1], send_sem.at[3], recv_sem.at[3],
-    )
 
     for x in range(E):
         lanes = slice(x * C, (x + 1) * C)
         mixed_ref[:, :, lanes] = mixed[x].astype(BF16)
         gfield_ref[:, :, lanes] = (upstream[x] + conv[x] * fluid[x]).astype(BF16)
-
-    wait_bytes(in3, recv_sem.at[3])
-    total = out3[...].astype(F32)
-    for step in range(NZ - 1):
-        total = total + in3[step].astype(F32)
+    stores[0].start()
+    stores[1].start()
+
+    wait_bytes(w_in3, recv_sem.at[2])
     mine = pl.ds(chip_y * PART, PART)
-    gather4[mine] = total.astype(BF16)
-    send_all(
-        NY, chip_y, in_y, lambda peer: gather4.at[mine],
-        lambda step: gather4.at[mine], send_sem.at[4], recv_sem.at[4],
-    )
-    wait_bytes(gather4.at[0 : (NY - 1) * PART], recv_sem.at[4])
-    gather5[sample] = gather4[0:SHARE]
-    send_all(
-        NS, sample, in_sample, lambda peer: gather5.at[sample],
-        lambda step: gather5.at[sample], send_sem.at[5], recv_sem.at[5],
-    )
-    wait_bytes(gather5.at[0 : NS - 1], recv_sem.at[5])
-
+    w_share[mine] = add_all(w_out3[...], w_in3, NZ - 1).astype(BF16)
+    send_all(
+        y_peers, lambda peer: w_share.at[mine], lambda slot: w_share.at[mine],
+        send_sem.at[3], recv_sem.at[3],
+    )
+
+    wait_bytes(k_in3, recv_sem.at[7])
+    k_all[sample] = add_all(k_out3[...], k_in3, NZ - 1).astype(BF16)
+    send_all(
+        x_peers, lambda peer: k_all.at[sample], lambda slot: k_all.at[sample],
+        send_sem.at[8], recv_sem.at[8],
+    )
+
+    wait_bytes(w_share.at[0 : (NY - 1) * PART], recv_sem.at[3])
+    w_all[sample] = w_share[0:W_SHARE]
+    send_all(
+        x_peers, lambda peer: w_all.at[sample], lambda slot: w_all.at[sample],
+        send_sem.at[4], recv_sem.at[4],
+    )
+
+    wait_bytes(k_all.at[0 : NS - 1], recv_sem.at[8])
     factor = 1.0 / math.sqrt(NS * layers * E**3)
 
+    rows = k_all[...].astype(F32).reshape(K_TILES * TILE, LANES)[:, 0:C] * factor
+    for pair in range(K * K):
+        gkernel_ref[pair // K, pair % K] = rows[pair * K : (pair + 1) * K]
+    stores[2].start()
+
+    wait_bytes(w_all.at[0 : NS - 1], recv_sem.at[4])
+
     def tile_of(index):
-        return gather5[index // W_SHARE, index % W_SHARE].astype(F32) * factor
+        return w_all[index // W_SHARE, index % W_SHARE].astype(F32) * factor
 
     for part in range(H // LANES):
         lanes = slice(part * LANES, (part + 1) * LANES)
@@ -382,17 +446,31 @@
             gwout_ref[row * TILE : (row + 1) * TILE, lanes] = tile_of(18 + 6 * part + row)
     last = tile_of(36)
     for part in range(H // LANES):
-        gbin_ref[0:1, part * LANES : (part + 1) * LANES] = last[part : part + 1]
+        gbin_ref[part : part + 1] = last[part : part + 1]
     gvec_ref[...] = last[3:7, 0:C]
-    rows = gather5[:, W_SHARE:SHARE].astype(F32).reshape(K_TILES * TILE, LANES)[:, 0:C] * factor
-    for pair in range(K * K):
-        gkernel_ref[pair // K, pair % K] = rows[pair * K : (pair + 1) * K]
+    for store in stores[3:]:
+        store.start()
 
     for side in range(2):
         wait_bytes(rims.at[side], halo_send.at[side])
         wait_bytes(grims.at[side], halo_send.at[2 + side])
-    for index, ref in enumerate((w_in1, k_in1, in2, in3, gather4.at[0 : (NY - 1) * PART], gather5.at[0 : NS - 1])):
+    sent = (
+        w_in1, w_in2, w_in3, w_share.at[0 : (NY - 1) * PART], w_all.at[0 : NS - 1],
+        k_in1, k_in2, k_in3, k_all.at[0 : NS - 1],
+    )
+    for index, ref in enumerate(sent):
         wait_bytes(ref, send_sem.at[index])
+    for store in stores:
+        store.wait()
+
+
+def write_out(*refs):
+    sources, dests, sem = refs[:7], refs[7:14], refs[14]
+    copies = [pltpu.make_async_copy(a, b, sem.at[i]) for i, (a, b) in enumerate(zip(sources, dests))]
+    for copy in copies:
+        copy.start()
+    for copy in copies:
+        copy.wait()
 
 
 def local(
@@ -402,14 +480,14 @@
     voxels = (E, E, E, C)
     spread = (K, E + 4, E + 4, E, C)
     rows = E**3
-    vmem = pl.BlockSpec(memory_space=pltpu.VMEM)
+    hbm = pl.BlockSpec(memory_space=pltpu.HBM)
     outs = (
         jax.ShapeDtypeStruct((E, E, E * C), BF16),
         jax.ShapeDtypeStruct((E, E, E * C), BF16),
         jax.ShapeDtypeStruct((K, K, K, C), F32),
         jax.ShapeDtypeStruct((C, H), F32),
         jax.ShapeDtypeStruct((C, H), F32),
-        jax.ShapeDtypeStruct((1, H), F32),
+        jax.ShapeDtypeStruct((H // LANES, LANES), F32),
         jax.ShapeDtypeStruct((4, C), F32),
     )
     scratch = [
@@ -434,29 +512,34 @@
         pltpu.VMEM((2, E, 2 * E, C), BF16),
         pltpu.VMEM((2, E, 2 * E, C), BF16),
         pltpu.VMEM((2, E, 2 * E, C), BF16),
-        pltpu.VMEM((W_TILES, TILE, LANES), BF16),
-        pltpu.VMEM((K_TILES, TILE, LANES), BF16),
-        pltpu.VMEM((NS - 1, W_SHARE, TILE, LANES), BF16),
-        pltpu.VMEM((NS - 1, K_SHARE, TILE, LANES), BF16),
-        pltpu.VMEM((NY * PART, TILE, LANES), BF16),
-        pltpu.VMEM((NY - 1, PART, TILE, LANES), BF16),
-        pltpu.VMEM((PART, TILE, LANES), BF16),
-        pltpu.VMEM((NZ - 1, PART, TILE, LANES), BF16),
-        pltpu.VMEM((NY * PART, TILE, LANES), BF16),
-        pltpu.VMEM((NS, SHARE, TILE, LANES), BF16),
+        *(pltpu.VMEM((*lead, TILE, LANES), BF16) for lead in (
+            (W_TILES,), (NS - 1, W_SHARE), (NY * PART,), (NY - 1, PART), (PART,), (NZ - 1, PART),
+            (NY * PART,), (NS, W_SHARE),
+            (K_TILES,), (NS - 1, K_SHARE), (K_SHARE,), (NY - 1, K_SHARE), (K_SHARE,),
+            (NZ - 1, K_SHARE), (NS, K_SHARE),
+        )),
+        *(pltpu.VMEM(shape, dtype) for shape, dtype in (
+            ((E, E, E * C), BF16), ((E, E * E), jnp.int32), ((1, NY * NZ), jnp.int32),
+            ((K, K, K, C), F32), ((1, C), F32), ((1, C), F32), ((C, H), BF16),
+            ((H // LANES, LANES), F32), ((C, H), BF16), ((1, C), F32), ((1, C), F32),
+            ((E, E, E * C), BF16),
+        )),
+        *(pltpu.VMEM(out.shape, out.dtype) for out in outs),
         pltpu.SemaphoreType.DMA((4,)),
         pltpu.SemaphoreType.DMA((4,)),
-        pltpu.SemaphoreType.DMA((6,)),
-        pltpu.SemaphoreType.DMA((6,)),
+        pltpu.SemaphoreType.DMA((9,)),
+        pltpu.SemaphoreType.DMA((9,)),
+        pltpu.SemaphoreType.DMA((12,)),
+        pltpu.SemaphoreType.DMA((7,)),
     ]
     results = pl.pallas_call(
         body,
         out_shape=outs,
-        in_specs=[vmem] * 12,
-        out_specs=[vmem] * 7,
+        in_specs=[hbm] * 12,
+        out_specs=[hbm] * 7,
         scratch_shapes=scratch,
         compiler_params=pltpu.CompilerParams(
-            collective_id=0, has_side_effects=True, vmem_limit_bytes=48 * 1024 * 1024
+            collective_id=0, has_side_effects=True, vmem_limit_bytes=VMEM_BYTES
         ),
         cost_estimate=pl.CostEstimate(flops=400_000_000, bytes_accessed=1_500_000, transcendentals=200_000),
         name="block_step",
@@ -468,14 +551,24 @@
         norm_gain[None],
         norm_bias[None],
         w_in,
-        b_in[None],
+        b_in.reshape(H // LANES, LANES),
         w_out.T,
         b_out[None],
         layer_scale[None],
         upstream[0, 0, 0],
     )
+    results = pl.pallas_call(
+        write_out,
+        out_shape=outs,
+        in_specs=[hbm] * 7,
+        out_specs=[hbm] * 7,
+        scratch_shapes=[pltpu.SemaphoreType.DMA((7,))],
+        compiler_params=pltpu.CompilerParams(vmem_limit_bytes=VMEM_BYTES),
+        cost_estimate=pl.CostEstimate(flops=0, bytes_accessed=1_000_000, transcendentals=0),
+        name="write_results",
+    )(*results)
     mixed, gfield, gkernel, gwin, gwout, gbin, gvec = results
-    return (mixed[None, None, None], gfield[None, None, None], gkernel, gwin, gwout.T, gbin[0], gvec)
+    return (mixed[None, None, None], gfield[None, None, None], gkernel, gwin, gwout.T, gbin.reshape(H), gvec)
 
 
 def solution(mesh):

time: 73.9 us -> 78.2 us (1.058)
  Pallas kernels: 62.6 us -> 77.4 us
  local copies, waits for them, and re-layouts: 9.66 us -> 0 us
    pallas_call x1 -> x2, Pallas kernels: 62.6 us -> 77.4 us  [the longest x1 59.3 us: local(): pl.pallas_call(body, out_shape=outs, in_specs=[hbm] * 12, out_specs=[hbm]...]
    unnamed x28 -> x0, local copies, waits for them, and re-layouts: 8.97 us -> none
where the time goes in v2:
time: 78.2 us; the launch traced here: 78 us
  Pallas kernels  77.4 us (99%)
    pallas_call x1, Pallas kernels, local(): pl.pallas_call(body, out_shape=outs, in_specs=[hbm] * 12, out_specs=[hbm]...  59.3 us
    pallas_call x1, Pallas kernels, local(): pl.pallas_call(write_out, out_shape=outs, in_specs=[hbm] * 7, out_specs=[...  18.1 us

profile of v2, /device:TPU:1, one launch (start us, length us, event | category | flops | bytes accessed | tf_op | source)
XLA Modules:
  0.0 78.0 jit_solution(10666144235353781371)
XLA Ops:
  0.6 59.3 %block_step.1 = (bf16[8,8,768]{2,1,0:T(8,128)(2,1)}, bf16[8,8,768]{2,1,0:T(8,128)(2,1)}, f32[5,5,5,96]{3,2,1,0:T(8,128)}, f32[96,384]{1,0:T(8,128)}, f32[96,384]...) custom-call(bf16[8,8,768]{2,1,0:T(8,128)(2,1)} %bitcast.15, s32[8,64]{1,0:T(8,128)} %bitcast.20, s32[1,128]{1,0:T(1,128)} %bitcast.23, ...), custom_call_target="tpu_custom_call" | custom-call | flops 400000000 | bytes 1500000 | tf_op jit(solution)/shard_map/block_step/pallas_call | solution.py:535
  59.9 18.1 %write_results.1 = (bf16[8,8,768]{2,1,0:T(8,128)(2,1)}, bf16[8,8,768]{2,1,0:T(8,128)(2,1)}, f32[5,5,5,96]{3,2,1,0:T(8,128)}, f32[96,384]{1,0:T(8,128)}, f32[96,3...) custom-call(bf16[8,8,768]{2,1,0:T(8,128)(2,1)} %get-tuple-element.21.refs_0_, ...), custom_call_target="tpu_custom_call" | custom-call | bytes 1000000 | tf_op jit(solution)/shard_map/write_results/pallas_call | solution.py:560

commit v3 on v2

--- a/solution.py
+++ b/solution.py
@@ -23,7 +23,7 @@
 NZ = 16
 NY = 8
 NS = 8
-ROWS = 2
+ROWS = 8
 TILE = 16
 LANES = 128
 W_TILES = 40
@@ -85,9 +85,10 @@
 
 
 def clear_sides(dest):
-    zeros = jnp.zeros((K, 2, E, E, C), F32)
-    dest[:, 0:2, 2 : 2 + E] = zeros
-    dest[:, 2 + E : 4 + E, 2 : 2 + E] = zeros
+    dest[:, 0:2, 2 : 2 + E] = jnp.zeros((K, 2, E, E, C), F32)
+    dest[:, 2 + E : 4 + E, 2 : 2 + E] = jnp.zeros((K, 2, E, E, C), F32)
+    dest[:, :, 0:2] = jnp.zeros((K, E + 4, 2, E, C), F32)
+    dest[:, :, 2 + E : 4 + E] = jnp.zeros((K, E + 4, 2, E, C), F32)
 
 
 def spread_halo(dest, halo, low, step_y, step_x, exists, y_index):
@@ -102,21 +103,37 @@
             dest[tap, first : first + count, low : low + 2] = block
 
 
-def conv_planes(field, weights, out, first, last, reverse):
-    def plane(index, carry):
-        z = lax.rem(index, E)
+def tap_row(weights, tap_z, tap_y, tap_x, reverse):
+    pair = tap_z * K + tap_y
+    return weights[K * K - 1 - pair, K - 1 - tap_x] if reverse else weights[pair, tap_x]
+
+
+def plane_sum(field, weights, total, z, tap_z, reverse):
+    for tap_y in range(K):
+        window = field[tap_y, :, z + tap_z]
+        for tap_x in range(K):
+            row = tap_row(weights, tap_z, tap_y, tap_x, reverse)
+            total = total + window[tap_x : tap_x + E] * row
+    return total
+
+
+def conv_own(field, weights, out, reverse):
+    def plane(z, carry):
         total = jnp.zeros((E, E, C), F32)
         for tap_z in range(K):
-            for tap_y in range(K):
-                window = field[tap_y, :, z + tap_z]
-                pair = tap_z * K + tap_y
-                for tap_x in range(K):
-                    row = weights[K * K - 1 - pair, K - 1 - tap_x] if reverse else weights[pair, tap_x]
-                    total = total + window[tap_x : tap_x + E] * row
+            total = plane_sum(field, weights, total, z, tap_z, reverse)
         out[:, z] = total
         return carry
 
-    lax.fori_loop(first, last, plane, 0)
+    lax.fori_loop(0, E, plane, 0)
+
+
+def conv_halo(field, weights, out, reverse):
+    for z, taps in ((0, (0, 1)), (1, (0,)), (6, (4,)), (7, (3, 4))):
+        total = out[:, z]
+        for tap_z in taps:
+            total = plane_sum(field, weights, total, z, tap_z, reverse)
+        out[:, z] = total
 
 
 def body(
@@ -197,31 +214,33 @@
         rims[0, x] = masked[E - 2 :].reshape(2 * E, C).astype(BF16)
         rims[1, x] = masked[:2].reshape(2 * E, C).astype(BF16)
 
+    clear_sides(padded)
+
+    def own_column(x, carry):
+        spread_own(padded, x, conv[x], y_index)
+        return carry
+
+    lax.fori_loop(0, E, own_column, 0)
+    loads[2].wait()
+
+    def spread_weights(pair, carry):
+        rows = dw_ref[pair // K, lax.rem(pair, K)]
+        weights[pair] = jnp.broadcast_to(rows[:, None, :], (K, E, C))
+        return carry
+
+    lax.fori_loop(0, K * K, spread_weights, 0)
+    conv_own(padded, weights, conv, False)
+
     pl.semaphore_wait(barrier, len(partners))
     send(rims.at[0], halos.at[0], halo_send.at[0], halo_recv.at[0], above)
     send(rims.at[1], halos.at[1], halo_send.at[1], halo_recv.at[1], below)
 
-    for load in loads[2:]:
+    for load in loads[3:]:
         load.wait()
     wide = up_ref[...].astype(F32)
     for x in range(E):
         upstream[x] = wide[:, :, x * C : (x + 1) * C]
-    clear_sides(padded)
     clear_sides(gpadded)
-
-    def own_column(x, carry):
-        spread_own(padded, x, conv[x], y_index)
-        return carry
-
-    lax.fori_loop(0, E, own_column, 0)
-
-    def spread_weights(pair, carry):
-        rows = dw_ref[pair // K, lax.rem(pair, K)]
-        weights[pair] = jnp.broadcast_to(rows[:, None, :], (K, E, C))
-        return carry
-
-    lax.fori_loop(0, K * K, spread_weights, 0)
-    conv_planes(padded, weights, conv, 2, 6, False)
 
     layer_index = lax.broadcasted_iota(jnp.int32, (1, layers), 1)
 
@@ -239,7 +258,7 @@
     for side in range(2):
         wait_bytes(halos.at[side], halo_recv.at[side])
     place_halos(padded, halos)
-    conv_planes(padded, weights, conv, 6, 10, False)
+    conv_halo(padded, weights, conv, False)
 
     vec_sum[...] = jnp.zeros_like(vec_sum)
     bin_sum[...] = jnp.zeros_like(bin_sum)
@@ -369,7 +388,7 @@
         lambda slot: w_in2.at[slot], send_sem.at[1], recv_sem.at[1],
     )
 
-    conv_planes(gpadded, weights, conv, 2, 6, True)
+    conv_own(gpadded, weights, conv, True)
 
     wait_bytes(k_in1, recv_sem.at[5])
     total = add_all(k_out1[pl.ds(sample * K_SHARE, K_SHARE)], k_in1, NS - 1)
@@ -395,7 +414,7 @@
         z_peers, lambda peer: k_out3, lambda slot: k_in3.at[slot], send_sem.at[7], recv_sem.at[7]
     )
 
-    conv_planes(gpadded, weights, conv, 6, 10, True)
+    conv_halo(gpadded, weights, conv, True)
 
     for x in range(E):
         lanes = slice(x * C, (x + 1) * C)
@@ -465,12 +484,16 @@
 
 
 def write_out(*refs):
-    sources, dests, sem = refs[:7], refs[7:14], refs[14]
-    copies = [pltpu.make_async_copy(a, b, sem.at[i]) for i, (a, b) in enumerate(zip(sources, dests))]
-    for copy in copies:
-        copy.start()
-    for copy in copies:
-        copy.wait()
+    sources, dests, held, sem = refs[:7], refs[7:14], refs[14:21], refs[21]
+    loads = [pltpu.make_async_copy(a, b, sem.at[0, i]) for i, (a, b) in enumerate(zip(sources, held))]
+    stores = [pltpu.make_async_copy(a, b, sem.at[1, i]) for i, (a, b) in enumerate(zip(held, dests))]
+    for load in loads:
+        load.start()
+    for load, store in zip(loads, stores):
+        load.wait()
+        store.start()
+    for store in stores:
+        store.wait()
 
 
 def local(
@@ -562,7 +585,10 @@
         out_shape=outs,
         in_specs=[hbm] * 7,
         out_specs=[hbm] * 7,
-        scratch_shapes=[pltpu.SemaphoreType.DMA((7,))],
+        scratch_shapes=[
+            *(pltpu.VMEM(out.shape, out.dtype) for out in outs),
+            pltpu.SemaphoreType.DMA((2, 7)),
+        ],
         compiler_params=pltpu.CompilerParams(vmem_limit_bytes=VMEM_BYTES),
         cost_estimate=pl.CostEstimate(flops=0, bytes_accessed=1_000_000, transcendentals=0),
         name="write_results",

time: 78.2 us -> 59.8 us (0.76)
  Pallas kernels: 77.4 us -> 59 us
    pallas_call x1, Pallas kernels: 18.1 us -> 1.9 us  [local(): pl.pallas_call(write_out, out_shape=outs, in_specs=[hbm] * 7, out_specs=[...]
    pallas_call x1, Pallas kernels: 59.3 us -> 57.1 us  [local(): pl.pallas_call(body, out_shape=outs, in_specs=[hbm] * 12, out_specs=[hbm]...]
where the time goes in v3:
time: 59.8 us; the launch traced here: 59.6 us
  Pallas kernels  59 us (99%)
  between operations  0.65 us (1%)
    pallas_call x1, Pallas kernels, local(): pl.pallas_call(body, out_shape=outs, in_specs=[hbm] * 12, out_specs=[hbm]...  57.1 us
    pallas_call x1, Pallas kernels, local(): pl.pallas_call(write_out, out_shape=outs, in_specs=[hbm] * 7, out_specs=[...  1.9 us

profile of v3, /device:TPU:1, one launch (start us, length us, event | category | flops | bytes accessed | tf_op | source)
XLA Modules:
  0.0 59.6 jit_solution(16463485687082191414)
XLA Ops:
  0.6 57.1 %block_step.1 = (bf16[8,8,768]{2,1,0:T(8,128)(2,1)}, bf16[8,8,768]{2,1,0:T(8,128)(2,1)}, f32[5,5,5,96]{3,2,1,0:T(8,128)}, f32[96,384]{1,0:T(8,128)}, f32[96,384]...) custom-call(bf16[8,8,768]{2,1,0:T(8,128)(2,1)} %bitcast.15, s32[8,64]{1,0:T(8,128)} %bitcast.20, s32[1,128]{1,0:T(1,128)} %bitcast.23, ...), custom_call_target="tpu_custom_call" | custom-call | flops 400000000 | bytes 1500000 | tf_op jit(solution)/shard_map/block_step/pallas_call | solution.py:558
  57.7 1.9 %write_results.1 = (bf16[8,8,768]{2,1,0:T(8,128)(2,1)}, bf16[8,8,768]{2,1,0:T(8,128)(2,1)}, f32[5,5,5,96]{3,2,1,0:T(8,128)}, f32[96,384]{1,0:T(8,128)}, f32[96,3...) custom-call(bf16[8,8,768]{2,1,0:T(8,128)(2,1)} %get-tuple-element.21.refs_0_, ...), custom_call_target="tpu_custom_call" | custom-call | bytes 1000000 | tf_op jit(solution)/shard_map/write_results/pallas_call | solution.py:583

commit v4 on v3

--- a/solution.py
+++ b/solution.py
@@ -87,8 +87,6 @@
 def clear_sides(dest):
     dest[:, 0:2, 2 : 2 + E] = jnp.zeros((K, 2, E, E, C), F32)
     dest[:, 2 + E : 4 + E, 2 : 2 + E] = jnp.zeros((K, 2, E, E, C), F32)
-    dest[:, :, 0:2] = jnp.zeros((K, E + 4, 2, E, C), F32)
-    dest[:, :, 2 + E : 4 + E] = jnp.zeros((K, E + 4, 2, E, C), F32)
 
 
 def spread_halo(dest, halo, low, step_y, step_x, exists, y_index):
@@ -118,14 +116,24 @@
 
 
 def conv_own(field, weights, out, reverse):
-    def plane(z, carry):
-        total = jnp.zeros((E, E, C), F32)
-        for tap_z in range(K):
-            total = plane_sum(field, weights, total, z, tap_z, reverse)
-        out[:, z] = total
-        return carry
-
-    lax.fori_loop(0, E, plane, 0)
+    def tap_layer(tap_z, first):
+        def plane(z, carry):
+            totals = [None] * E
+            for tap_y in range(K):
+                window = field[tap_y, 2 : 2 + E, z + tap_z]
+                for tap_x in range(K):
+                    row = tap_row(weights, tap_z, tap_y, tap_x, reverse)
+                    for x in range(max(0, 2 - tap_x), min(E, E + 2 - tap_x)):
+                        term = window[x + tap_x - 2] * row
+                        totals[x] = term if totals[x] is None else totals[x] + term
+            for x in range(E):
+                out[x, z] = totals[x] if first else out[x, z] + totals[x]
+            return carry
+
+        lax.fori_loop(max(0, 2 - tap_z), min(E, E + 2 - tap_z), plane, 0)
+
+    for tap_z in (2, 0, 1, 3, 4):
+        tap_layer(tap_z, tap_z == 2)
 
 
 def conv_halo(field, weights, out, reverse):
@@ -148,7 +156,7 @@
     field_ref, wall_ref, pos_ref, dw_ref, gain_ref, bias_ref, win_ref, bin_ref, wout_ref, bout_ref,
     scale_ref, up_ref,
     mixed_ref, gfield_ref, gkernel_ref, gwin_ref, gwout_ref, gbin_ref, gvec_ref,
-    halo_send, halo_recv, send_sem, recv_sem, load_sem, store_sem,
+    halo_send, halo_recv, send_sem, recv_sem, load_sem, store_sem, ready,
 ):
     stores = [
         pltpu.make_async_copy(source, dest, store_sem.at[index])
@@ -189,10 +197,27 @@
         index = lax.rem(chip_z + step, NZ)
         z_peers.append((index, (chip_y * NZ + index, sample)))
 
+    def ring_pair(distance):
+        pair = []
+        if distance < NZ // 2:
+            for step in (distance, NZ - distance):
+                pair.append((chip_y * NZ + lax.rem(chip_z + step, NZ), sample))
+        if distance < NY // 2:
+            for step in (distance, NY - distance):
+                pair.append((lax.rem(chip_y + step, NY) * NZ + chip_z, sample))
+        return pair
+
     barrier = pltpu.get_barrier_semaphore()
-    partners = [above, below] + [device for _, device in x_peers + y_peers + z_peers]
-    for device in partners:
+    near = [above, below] + ring_pair(1) + [device for _, device in x_peers]
+    for device in near:
         pl.semaphore_signal(barrier, inc=1, device_id=device, device_id_type=MESH)
+
+    def tell(turn):
+        for device in ring_pair(2**turn):
+            pl.semaphore_signal(ready.at[turn], inc=1, device_id=device, device_id_type=MESH)
+
+    def hear(turn):
+        pl.semaphore_wait(ready.at[turn], len(ring_pair(2**turn)))
 
     loads[0].wait()
     loads[1].wait()
@@ -214,6 +239,11 @@
         rims[0, x] = masked[E - 2 :].reshape(2 * E, C).astype(BF16)
         rims[1, x] = masked[:2].reshape(2 * E, C).astype(BF16)
 
+    pl.semaphore_wait(barrier, len(near))
+    send(rims.at[0], halos.at[0], halo_send.at[0], halo_recv.at[0], above)
+    send(rims.at[1], halos.at[1], halo_send.at[1], halo_recv.at[1], below)
+    tell(0)
+
     clear_sides(padded)
 
     def own_column(x, carry):
@@ -231,16 +261,14 @@
     lax.fori_loop(0, K * K, spread_weights, 0)
     conv_own(padded, weights, conv, False)
 
-    pl.semaphore_wait(barrier, len(partners))
-    send(rims.at[0], halos.at[0], halo_send.at[0], halo_recv.at[0], above)
-    send(rims.at[1], halos.at[1], halo_send.at[1], halo_recv.at[1], below)
+    hear(0)
+    tell(1)
 
     for load in loads[3:]:
         load.wait()
     wide = up_ref[...].astype(F32)
     for x in range(E):
         upstream[x] = wide[:, :, x * C : (x + 1) * C]
-    clear_sides(gpadded)
 
     layer_index = lax.broadcasted_iota(jnp.int32, (1, layers), 1)
 
@@ -348,6 +376,8 @@
         x_peers, lambda peer: w_out1.at[pl.ds(peer * W_SHARE, W_SHARE)],
         lambda slot: w_in1.at[slot], send_sem.at[0], recv_sem.at[0],
     )
+    hear(1)
+    tell(2)
 
     kernel_rows[...] = jnp.zeros_like(kernel_rows)
 
@@ -400,6 +430,7 @@
     wait_bytes(w_in2, recv_sem.at[1])
     total = add_all(w_out2[pl.ds(chip_y * PART, PART)], w_in2, NY - 1)
     w_out3[...] = total.astype(BF16)
+    hear(2)
     send_all(
         z_peers, lambda peer: w_out3, lambda slot: w_in3.at[slot], send_sem.at[2], recv_sem.at[2]
     )
@@ -554,6 +585,7 @@
         pltpu.SemaphoreType.DMA((9,)),
         pltpu.SemaphoreType.DMA((12,)),
         pltpu.SemaphoreType.DMA((7,)),
+        pltpu.SemaphoreType.REGULAR((3,)),
     ]
     results = pl.pallas_call(
         body,

time: 59.8 us -> 54.2 us (0.906)
  Pallas kernels: 59 us -> 53.3 us
    pallas_call x1, Pallas kernels: 57.1 us -> 51.4 us  [local(): pl.pallas_call(body, out_shape=outs, in_specs=[hbm] * 12, out_specs=[hbm]...]
where the time goes in v4:
time: 54.2 us; the launch traced here: 54 us
  Pallas kernels  53.3 us (98%)
  between operations  0.65 us (1%)
    pallas_call x1, Pallas kernels, local(): pl.pallas_call(body, out_shape=outs, in_specs=[hbm] * 12, out_specs=[hbm]...  51.4 us
    pallas_call x1, Pallas kernels, local(): pl.pallas_call(write_out, out_shape=outs, in_specs=[hbm] * 7, out_specs=[...  1.9 us

profile of v4, /device:TPU:1, one launch (start us, length us, event | category | flops | bytes accessed | tf_op | source)
XLA Modules:
  0.0 54.0 jit_solution(12724355567542316685)
XLA Ops:
  0.6 51.4 %block_step.1 = (bf16[8,8,768]{2,1,0:T(8,128)(2,1)}, bf16[8,8,768]{2,1,0:T(8,128)(2,1)}, f32[5,5,5,96]{3,2,1,0:T(8,128)}, f32[96,384]{1,0:T(8,128)}, f32[96,384]...) custom-call(bf16[8,8,768]{2,1,0:T(8,128)(2,1)} %bitcast.15, s32[8,64]{1,0:T(8,128)} %bitcast.20, s32[1,128]{1,0:T(1,128)} %bitcast.23, ...), custom_call_target="tpu_custom_call" | custom-call | flops 400000000 | bytes 1500000 | tf_op jit(solution)/shard_map/block_step/pallas_call | solution.py:590
  52.1 1.9 %write_results.1 = (bf16[8,8,768]{2,1,0:T(8,128)(2,1)}, bf16[8,8,768]{2,1,0:T(8,128)(2,1)}, f32[5,5,5,96]{3,2,1,0:T(8,128)}, f32[96,384]{1,0:T(8,128)}, f32[96,3...) custom-call(bf16[8,8,768]{2,1,0:T(8,128)(2,1)} %get-tuple-element.21.refs_0_, ...), custom_call_target="tpu_custom_call" | custom-call | bytes 1000000 | tf_op jit(solution)/shard_map/write_results/pallas_call | solution.py:615

commit v5 on v4

--- a/solution.py
+++ b/solution.py
@@ -23,7 +23,6 @@
 NZ = 16
 NY = 8
 NS = 8
-ROWS = 8
 TILE = 16
 LANES = 128
 W_TILES = 40
@@ -31,6 +30,7 @@
 W_SHARE = W_TILES // NS
 K_SHARE = K_TILES // NS
 PART = -(-W_SHARE // NY)
+PARAM_SCALE = 1.0 / math.sqrt(NS * NY * NZ * E**3)
 
 
 def wait_bytes(ref, sem):
@@ -147,22 +147,21 @@
 def body(
     field_hbm, wall_hbm, pos_hbm, dw_hbm, gain_hbm, bias_hbm, win_hbm, bin_hbm, wout_hbm, bout_hbm,
     scale_hbm, up_hbm,
-    mixed_hbm, gfield_hbm, gkernel_hbm, gwin_hbm, gwout_hbm, gbin_hbm, gvec_hbm,
+    mixed_hbm, gfield_hbm, gkernel_hbm, w_hbm,
     weights, padded, gpadded, conv, grad, fluid, field, upstream, mixed,
     normed_all, act_all, gpre_all, gbranch_all, vec_sum, bin_sum, kernel_rows, vec_tile,
     rims, halos, grims, ghalos,
-    w_out1, w_in1, w_out2, w_in2, w_out3, w_in3, w_share, w_all,
+    w_out1, w_in1, w_out2, w_in2, w_out3, w_in3, w_share,
     k_out1, k_in1, k_out2, k_in2, k_out3, k_in3, k_all,
     field_ref, wall_ref, pos_ref, dw_ref, gain_ref, bias_ref, win_ref, bin_ref, wout_ref, bout_ref,
     scale_ref, up_ref,
-    mixed_ref, gfield_ref, gkernel_ref, gwin_ref, gwout_ref, gbin_ref, gvec_ref,
+    mixed_ref, gfield_ref, gkernel_ref,
     halo_send, halo_recv, send_sem, recv_sem, load_sem, store_sem, ready,
 ):
     stores = [
         pltpu.make_async_copy(source, dest, store_sem.at[index])
         for index, (source, dest) in enumerate((
             (mixed_ref, mixed_hbm), (gfield_ref, gfield_hbm), (gkernel_ref, gkernel_hbm),
-            (gwin_ref, gwin_hbm), (gwout_ref, gwout_hbm), (gbin_ref, gbin_hbm), (gvec_ref, gvec_hbm),
         ))
     ]
     loads = [
@@ -288,76 +287,51 @@
     place_halos(padded, halos)
     conv_halo(padded, weights, conv, False)
 
-    vec_sum[...] = jnp.zeros_like(vec_sum)
-    bin_sum[...] = jnp.zeros_like(bin_sum)
     b_in = jnp.concatenate([bin_ref[part : part + 1] for part in range(H // LANES)], axis=1)
     gain, bias, bout, scale = gain_ref[...], bias_ref[...], bout_ref[...], scale_ref[...]
-    count = ROWS * E * E
+    count = E * E * E
 
     def by_sublane(values):
         return jnp.sum(values.reshape(count // E, E, values.shape[1]), axis=0)
 
-    def dense(step, carry):
-        columns = pl.ds(step * ROWS, ROWS)
-        rows = pl.ds(pl.multiple_of(step * count, count), count)
-        conv_rows = conv[columns].reshape(count, C)
-        row_mean = jnp.mean(conv_rows, axis=1, keepdims=True)
-        centred = conv_rows - row_mean
-        row_var = jnp.mean(centred * centred, axis=1, keepdims=True)
-        inv_std = lax.rsqrt(row_var + NORM_EPS)
-        unit_rows = centred * inv_std
-        normed = (unit_rows * gain + bias).astype(BF16)
-        pre_act = jnp.dot(normed, win_ref[...], preferred_element_type=F32) + b_in
-        square = pre_act * pre_act
-        tanh_value = jnp.tanh(GELU_SCALE * (pre_act + GELU_CUBIC * square * pre_act))
-        half = 0.5 * (1.0 + tanh_value)
-        activated = (pre_act * half).astype(BF16)
-        slope = half + 0.5 * pre_act * (1.0 - tanh_value * tanh_value) * (
-            GELU_SCALE * (1.0 + 3.0 * GELU_CUBIC * square)
+    conv_rows = conv[...].reshape(count, C)
+    row_mean = jnp.mean(conv_rows, axis=1, keepdims=True)
+    centred = conv_rows - row_mean
+    row_var = jnp.mean(centred * centred, axis=1, keepdims=True)
+    inv_std = lax.rsqrt(row_var + NORM_EPS)
+    unit_rows = centred * inv_std
+    normed = (unit_rows * gain + bias).astype(BF16)
+    pre_act = jnp.dot(normed, win_ref[...], preferred_element_type=F32) + b_in
+    square = pre_act * pre_act
+    tanh_value = jnp.tanh(GELU_SCALE * (pre_act + GELU_CUBIC * square * pre_act))
+    half = 0.5 * (1.0 + tanh_value)
+    activated = (pre_act * half).astype(BF16)
+    slope = half + 0.5 * pre_act * (1.0 - tanh_value * tanh_value) * (
+        GELU_SCALE * (1.0 + 3.0 * GELU_CUBIC * square)
+    )
+    branch = (
+        lax.dot_general(
+            activated, wout_ref[...], (((1,), (1,)), ((), ())), preferred_element_type=F32
         )
-        branch = (
-            lax.dot_general(
-                activated, wout_ref[...], (((1,), (1,)), ((), ())), preferred_element_type=F32
-            )
-            + bout
-        )
-        mixed[columns] = (field[columns].reshape(count, C) + scale * branch).reshape(ROWS, E, E, C)
-        seed = upstream[columns].reshape(count, C)
-        grad_branch = (seed * scale).astype(BF16)
-        grad_act = jnp.dot(grad_branch, wout_ref[...], preferred_element_type=F32)
-        grad_pre = (grad_act * slope).astype(BF16)
-        grad_normed = lax.dot_general(
-            grad_pre, win_ref[...], (((1,), (1,)), ((), ())), preferred_element_type=F32
-        )
-        scaled = grad_normed * gain
-        grad_conv = inv_std * (
-            scaled
-            - jnp.mean(scaled, axis=1, keepdims=True)
-            - unit_rows * jnp.mean(scaled * unit_rows, axis=1, keepdims=True)
-        )
-        grad[columns] = grad_conv.astype(BF16).astype(F32).reshape(ROWS, E, E, C)
-        normed_all[rows] = normed
-        act_all[rows] = activated
-        gpre_all[rows] = grad_pre
-        gbranch_all[rows] = grad_branch
-        vec_sum[0] += by_sublane(grad_normed * unit_rows)
-        vec_sum[1] += by_sublane(grad_normed)
-        vec_sum[2] += by_sublane(grad_branch.astype(F32))
-        vec_sum[3] += by_sublane(seed * branch)
-        bin_sum[...] += by_sublane(grad_pre.astype(F32))
-        return carry
-
-    lax.fori_loop(0, E // ROWS, dense, 0)
-
-    def grad_rims(x, carry):
-        grims[0, x] = grad[x, E - 2 :].reshape(2 * E, C).astype(BF16)
-        grims[1, x] = grad[x, :2].reshape(2 * E, C).astype(BF16)
-        return carry
-
-    lax.fori_loop(0, E, grad_rims, 0)
-    send(grims.at[0], ghalos.at[0], halo_send.at[2], halo_recv.at[2], above)
-    send(grims.at[1], ghalos.at[1], halo_send.at[3], halo_recv.at[3], below)
-
+        + bout
+    )
+    mixed[...] = (field[...].reshape(count, C) + scale * branch).reshape(E, E, E, C)
+    seed = upstream[...].reshape(count, C)
+    grad_branch = (seed * scale).astype(BF16)
+    grad_act = jnp.dot(grad_branch, wout_ref[...], preferred_element_type=F32)
+    grad_pre = (grad_act * slope).astype(BF16)
+    grad_normed = lax.dot_general(
+        grad_pre, win_ref[...], (((1,), (1,)), ((), ())), preferred_element_type=F32
+    )
+    normed_all[...] = normed
+    act_all[...] = activated
+    gpre_all[...] = grad_pre
+    gbranch_all[...] = grad_branch
+    vec_sum[0] = by_sublane(grad_normed * unit_rows)
+    vec_sum[1] = by_sublane(grad_normed)
+    vec_sum[2] = by_sublane(grad_branch.astype(F32))
+    vec_sum[3] = by_sublane(seed * branch)
+    bin_sum[...] = by_sublane(grad_pre.astype(F32))
     by_rows = (((0,), (0,)), ((), ()))
     for base, left, right in ((0, normed_all, gpre_all), (18, gbranch_all, act_all)):
         product = lax.dot_general(left[...], right[...], by_rows, preferred_element_type=F32)
@@ -379,34 +353,51 @@
     hear(1)
     tell(2)
 
+    scaled = grad_normed * gain
+    grad_conv = inv_std * (
+        scaled
+        - jnp.mean(scaled, axis=1, keepdims=True)
+        - unit_rows * jnp.mean(scaled * unit_rows, axis=1, keepdims=True)
+    )
+    grad[...] = grad_conv.astype(BF16).astype(F32).reshape(E, E, E, C)
+
+    def grad_rims(x, carry):
+        grims[0, x] = grad[x, E - 2 :].reshape(2 * E, C).astype(BF16)
+        grims[1, x] = grad[x, :2].reshape(2 * E, C).astype(BF16)
+        return carry
+
+    lax.fori_loop(0, E, grad_rims, 0)
+    send(grims.at[0], ghalos.at[0], halo_send.at[2], halo_recv.at[2], above)
+    send(grims.at[1], ghalos.at[1], halo_send.at[3], halo_recv.at[3], below)
+
+
     kernel_rows[...] = jnp.zeros_like(kernel_rows)
 
-    def kernel_pair(pair, carry):
-        tap_z = pair // K
-        tap_y = lax.rem(pair, K)
-        sums = [jnp.zeros((E, C), F32) for _ in range(K)]
-        for z in range(E):
-            window = padded[tap_y, :, z + tap_z]
-            factor = grad[:, z]
+    def kernel_layer(tap_z):
+        def kernel_pair(tap_y, carry):
+            sums = [jnp.zeros((E, C), F32) for _ in range(K)]
+            for z in range(E):
+                window = padded[tap_y, :, z + tap_z]
+                factor = grad[:, z]
+                own = 2 <= z + tap_z < 2 + E
+                for tap_x in range(K):
+                    low, high = (max(0, 2 - tap_x), min(E, E + 2 - tap_x)) if own else (0, E)
+                    product = window[low + tap_x : high + tap_x] * factor[low:high]
+                    sums[tap_x] = sums[tap_x] + jnp.sum(product, axis=0)
             for tap_x in range(K):
-                sums[tap_x] = sums[tap_x] + jnp.sum(window[tap_x : tap_x + E] * factor, axis=0)
-        for tap_x in range(K):
-            total = jnp.sum(sums[tap_x], axis=0, keepdims=True)
-            kernel_rows[pl.ds(pair * K + tap_x, 1), 0:C] = total
-        return carry
-
-    lax.fori_loop(0, K * K, kernel_pair, 0)
+                total = jnp.sum(sums[tap_x], axis=0, keepdims=True)
+                kernel_rows[pl.ds((tap_z * K + tap_y) * K + tap_x, 1), 0:C] = total
+            return carry
+
+        lax.fori_loop(0, K, kernel_pair, 0)
+
+    for tap_z in range(K):
+        kernel_layer(tap_z)
     k_out1[...] = kernel_rows[...].astype(BF16).reshape(K_TILES, TILE, LANES)
     send_all(
         x_peers, lambda peer: k_out1.at[pl.ds(peer * K_SHARE, K_SHARE)],
         lambda slot: k_in1.at[slot], send_sem.at[5], recv_sem.at[5],
     )
-
-    def own_grad_column(x, carry):
-        spread_own(gpadded, x, grad[x], y_index)
-        return carry
-
-    lax.fori_loop(0, E, own_grad_column, 0)
 
     wait_bytes(w_in1, recv_sem.at[0])
     total = add_all(w_out1[pl.ds(sample * W_SHARE, W_SHARE)], w_in1, NS - 1)
@@ -417,6 +408,12 @@
         y_peers, lambda peer: w_out2.at[pl.ds(peer * PART, PART)],
         lambda slot: w_in2.at[slot], send_sem.at[1], recv_sem.at[1],
     )
+
+    def own_grad_column(x, carry):
+        spread_own(gpadded, x, grad[x], y_index)
+        return carry
+
+    lax.fori_loop(0, E, own_grad_column, 0)
 
     conv_own(gpadded, weights, conv, True)
 
@@ -470,61 +467,65 @@
     )
 
     wait_bytes(w_share.at[0 : (NY - 1) * PART], recv_sem.at[3])
-    w_all[sample] = w_share[0:W_SHARE]
-    send_all(
-        x_peers, lambda peer: w_all.at[sample], lambda slot: w_all.at[sample],
+    mine = w_hbm.at[pl.ds(sample * W_SHARE, W_SHARE)]
+    send_all(
+        x_peers, lambda peer: w_share.at[0:W_SHARE], lambda slot: mine,
         send_sem.at[4], recv_sem.at[4],
     )
+    keep = pltpu.make_async_copy(w_share.at[0:W_SHARE], mine, store_sem.at[3])
+    keep.start()
 
     wait_bytes(k_all.at[0 : NS - 1], recv_sem.at[8])
-    factor = 1.0 / math.sqrt(NS * layers * E**3)
-
-    rows = k_all[...].astype(F32).reshape(K_TILES * TILE, LANES)[:, 0:C] * factor
+    rows = k_all[...].astype(F32).reshape(K_TILES * TILE, LANES)[:, 0:C] * PARAM_SCALE
     for pair in range(K * K):
         gkernel_ref[pair // K, pair % K] = rows[pair * K : (pair + 1) * K]
     stores[2].start()
-
-    wait_bytes(w_all.at[0 : NS - 1], recv_sem.at[4])
-
-    def tile_of(index):
-        return w_all[index // W_SHARE, index % W_SHARE].astype(F32) * factor
-
-    for part in range(H // LANES):
-        lanes = slice(part * LANES, (part + 1) * LANES)
-        for row in range(6):
-            gwin_ref[row * TILE : (row + 1) * TILE, lanes] = tile_of(6 * part + row)
-            gwout_ref[row * TILE : (row + 1) * TILE, lanes] = tile_of(18 + 6 * part + row)
-    last = tile_of(36)
-    for part in range(H // LANES):
-        gbin_ref[part : part + 1] = last[part : part + 1]
-    gvec_ref[...] = last[3:7, 0:C]
-    for store in stores[3:]:
-        store.start()
 
     for side in range(2):
         wait_bytes(rims.at[side], halo_send.at[side])
         wait_bytes(grims.at[side], halo_send.at[2 + side])
     sent = (
-        w_in1, w_in2, w_in3, w_share.at[0 : (NY - 1) * PART], w_all.at[0 : NS - 1],
+        w_in1, w_in2, w_in3, w_share.at[0 : (NY - 1) * PART], w_hbm.at[0 : (NS - 1) * W_SHARE],
         k_in1, k_in2, k_in3, k_all.at[0 : NS - 1],
     )
     for index, ref in enumerate(sent):
         wait_bytes(ref, send_sem.at[index])
     for store in stores:
         store.wait()
-
-
-def write_out(*refs):
-    sources, dests, held, sem = refs[:7], refs[7:14], refs[14:21], refs[21]
-    loads = [pltpu.make_async_copy(a, b, sem.at[0, i]) for i, (a, b) in enumerate(zip(sources, held))]
-    stores = [pltpu.make_async_copy(a, b, sem.at[1, i]) for i, (a, b) in enumerate(zip(held, dests))]
+    keep.wait()
+    wait_bytes(w_hbm.at[0 : (NS - 1) * W_SHARE], recv_sem.at[4])
+
+
+def write_out(
+    mixed_in, gfield_in, gkernel_in, tiles_in,
+    mixed_out, gfield_out, gkernel_out, gwin_out, gwout_out, gbin_out, gvec_out,
+    mixed, gfield, gkernel, gwin, gwout, gbin, gvec, tiles, sem,
+):
+    def copies(pairs, first):
+        return [pltpu.make_async_copy(a, b, sem.at[first + i]) for i, (a, b) in enumerate(pairs)]
+
+    load_tiles, = copies([(tiles_in, tiles)], 0)
+    loads = copies([(mixed_in, mixed), (gfield_in, gfield), (gkernel_in, gkernel)], 1)
+    passed = copies([(mixed, mixed_out), (gfield, gfield_out), (gkernel, gkernel_out)], 4)
+    made = copies([(gwin, gwin_out), (gwout, gwout_out), (gbin, gbin_out), (gvec, gvec_out)], 7)
+    load_tiles.start()
     for load in loads:
         load.start()
-    for load, store in zip(loads, stores):
+    load_tiles.wait()
+    for base, dest in ((0, gwin), (18, gwout)):
+        for part in range(H // LANES):
+            block = tiles[base + 6 * part : base + 6 * part + 6].astype(F32) * PARAM_SCALE
+            dest[:, part * LANES : (part + 1) * LANES] = block.reshape(C, LANES)
+    last = tiles[36].astype(F32) * PARAM_SCALE
+    gbin[...] = last[0:3]
+    gvec[...] = last[3:7, 0:C]
+    for copy in made:
+        copy.start()
+    for load, copy in zip(loads, passed):
         load.wait()
-        store.start()
-    for store in stores:
-        store.wait()
+        copy.start()
+    for copy in passed + made:
+        copy.wait()
 
 
 def local(
@@ -568,7 +569,7 @@
         pltpu.VMEM((2, E, 2 * E, C), BF16),
         *(pltpu.VMEM((*lead, TILE, LANES), BF16) for lead in (
             (W_TILES,), (NS - 1, W_SHARE), (NY * PART,), (NY - 1, PART), (PART,), (NZ - 1, PART),
-            (NY * PART,), (NS, W_SHARE),
+            (NY * PART,),
             (K_TILES,), (NS - 1, K_SHARE), (K_SHARE,), (NY - 1, K_SHARE), (K_SHARE,),
             (NZ - 1, K_SHARE), (NS, K_SHARE),
         )),
@@ -578,20 +579,20 @@
             ((H // LANES, LANES), F32), ((C, H), BF16), ((1, C), F32), ((1, C), F32),
             ((E, E, E * C), BF16),
         )),
-        *(pltpu.VMEM(out.shape, out.dtype) for out in outs),
+        *(pltpu.VMEM(out.shape, out.dtype) for out in outs[:3]),
         pltpu.SemaphoreType.DMA((4,)),
         pltpu.SemaphoreType.DMA((4,)),
         pltpu.SemaphoreType.DMA((9,)),
         pltpu.SemaphoreType.DMA((9,)),
         pltpu.SemaphoreType.DMA((12,)),
-        pltpu.SemaphoreType.DMA((7,)),
+        pltpu.SemaphoreType.DMA((4,)),
         pltpu.SemaphoreType.REGULAR((3,)),
     ]
     results = pl.pallas_call(
         body,
-        out_shape=outs,
+        out_shape=outs[:3] + (jax.ShapeDtypeStruct((W_TILES, TILE, LANES), BF16),),
         in_specs=[hbm] * 12,
-        out_specs=[hbm] * 7,
+        out_specs=[hbm] * 4,
         scratch_shapes=scratch,
         compiler_params=pltpu.CompilerParams(
             collective_id=0, has_side_effects=True, vmem_limit_bytes=VMEM_BYTES
@@ -615,11 +616,12 @@
     results = pl.pallas_call(
         write_out,
         out_shape=outs,
-        in_specs=[hbm] * 7,
+        in_specs=[hbm] * 4,
         out_specs=[hbm] * 7,
         scratch_shapes=[
             *(pltpu.VMEM(out.shape, out.dtype) for out in outs),
-            pltpu.SemaphoreType.DMA((2, 7)),
+            pltpu.VMEM((W_TILES, TILE, LANES), BF16),
+            pltpu.SemaphoreType.DMA((11,)),
         ],
         compiler_params=pltpu.CompilerParams(vmem_limit_bytes=VMEM_BYTES),
         cost_estimate=pl.CostEstimate(flops=0, bytes_accessed=1_000_000, transcendentals=0),

time: 54.2 us -> 52.7 us (0.972)
  Pallas kernels: 53.3 us -> 51.9 us
    pallas_call x2, Pallas kernels: 53.3 us -> 51.9 us  [the longest x1 50.1 us: local(): pl.pallas_call(body, out_shape=outs[:3] + (jax.ShapeDtypeStruct((W_TILES,...]
where the time goes in v5:
time: 52.7 us; the launch traced here: 52.6 us
  Pallas kernels  51.9 us (98%)
  between operations  0.65 us (1%)
    pallas_call x1, Pallas kernels, local(): pl.pallas_call(body, out_shape=outs[:3] + (jax.ShapeDtypeStruct((W_TILES,...  50.1 us
    pallas_call x1, Pallas kernels, local(): pl.pallas_call(write_out, out_shape=outs, in_specs=[hbm] * 4, out_specs=[...  1.83 us

profile of v5, /device:TPU:1, one launch (start us, length us, event | category | flops | bytes accessed | tf_op | source)
XLA Modules:
  0.0 52.6 jit_solution(10719067777297668178)
XLA Ops:
  0.6 50.1 %block_step.1 = (bf16[8,8,768]{2,1,0:T(8,128)(2,1)}, bf16[8,8,768]{2,1,0:T(8,128)(2,1)}, f32[5,5,5,96]{3,2,1,0:T(8,128)}, bf16[40,16,128]{2,1,0:T(8,128)(2,1)}) custom-call(bf16[8,8,768]{2,1,0:T(8,128)(2,1)} %bitcast.15, s32[8,64]{1,0:T(8,128)} %bitcast.20, s32[1,128]{1,0:T(1,128)} %bitcast.23, f32[5,5,5,96]{3,2,1,0:T(8,128)} %dw_hbm.1, f32[1,96]{1,0:T(1,128)} %bitcast.24, ...), custom_call_target="tpu_custom_call" | custom-call | flops 400000000 | bytes 1500000 | tf_op jit(solution)/shard_map/block_step/pallas_call | solution.py:591
  50.7 1.8 %write_results.1 = (bf16[8,8,768]{2,1,0:T(8,128)(2,1)}, bf16[8,8,768]{2,1,0:T(8,128)(2,1)}, f32[5,5,5,96]{3,2,1,0:T(8,128)}, f32[96,384]{1,0:T(8,128)}, f32[96,3...) custom-call(bf16[8,8,768]{2,1,0:T(8,128)(2,1)} %get-tuple-element.18.mixed_in, ...), custom_call_target="tpu_custom_call" | custom-call | bytes 1000000 | tf_op jit(solution)/shard_map/write_results/pallas_call | solution.py:616

commit v6 on v5

--- a/solution.py
+++ b/solution.py
@@ -147,21 +147,21 @@
 def body(
     field_hbm, wall_hbm, pos_hbm, dw_hbm, gain_hbm, bias_hbm, win_hbm, bin_hbm, wout_hbm, bout_hbm,
     scale_hbm, up_hbm,
-    mixed_hbm, gfield_hbm, gkernel_hbm, w_hbm,
+    mixed_hbm, gfield_hbm, k_hbm, w_hbm,
     weights, padded, gpadded, conv, grad, fluid, field, upstream, mixed,
     normed_all, act_all, gpre_all, gbranch_all, vec_sum, bin_sum, kernel_rows, vec_tile,
     rims, halos, grims, ghalos,
     w_out1, w_in1, w_out2, w_in2, w_out3, w_in3, w_share,
-    k_out1, k_in1, k_out2, k_in2, k_out3, k_in3, k_all,
+    k_out1, k_in1, k_out2, k_in2, k_out3, k_in3, k_share,
     field_ref, wall_ref, pos_ref, dw_ref, gain_ref, bias_ref, win_ref, bin_ref, wout_ref, bout_ref,
     scale_ref, up_ref,
-    mixed_ref, gfield_ref, gkernel_ref,
+    mixed_ref, gfield_ref,
     halo_send, halo_recv, send_sem, recv_sem, load_sem, store_sem, ready,
 ):
     stores = [
         pltpu.make_async_copy(source, dest, store_sem.at[index])
         for index, (source, dest) in enumerate((
-            (mixed_ref, mixed_hbm), (gfield_ref, gfield_hbm), (gkernel_ref, gkernel_hbm),
+            (mixed_ref, mixed_hbm), (gfield_ref, gfield_hbm),
         ))
     ]
     loads = [
@@ -374,22 +374,22 @@
     kernel_rows[...] = jnp.zeros_like(kernel_rows)
 
     def kernel_layer(tap_z):
-        def kernel_pair(tap_y, carry):
-            sums = [jnp.zeros((E, C), F32) for _ in range(K)]
+        for group in ((0, 1), (2, 3), (4,)):
+            sums = {}
             for z in range(E):
-                window = padded[tap_y, :, z + tap_z]
                 factor = grad[:, z]
                 own = 2 <= z + tap_z < 2 + E
-                for tap_x in range(K):
-                    low, high = (max(0, 2 - tap_x), min(E, E + 2 - tap_x)) if own else (0, E)
-                    product = window[low + tap_x : high + tap_x] * factor[low:high]
-                    sums[tap_x] = sums[tap_x] + jnp.sum(product, axis=0)
-            for tap_x in range(K):
-                total = jnp.sum(sums[tap_x], axis=0, keepdims=True)
-                kernel_rows[pl.ds((tap_z * K + tap_y) * K + tap_x, 1), 0:C] = total
-            return carry
-
-        lax.fori_loop(0, K, kernel_pair, 0)
+                for tap_y in group:
+                    window = padded[tap_y, :, z + tap_z]
+                    for tap_x in range(K):
+                        low, high = (max(0, 2 - tap_x), min(E, E + 2 - tap_x)) if own else (0, E)
+                        part = window[low + tap_x : high + tap_x] * factor[low:high]
+                        part = jnp.sum(part, axis=0)
+                        tap = (tap_y, tap_x)
+                        sums[tap] = sums[tap] + part if tap in sums else part
+            for (tap_y, tap_x), total in sums.items():
+                row = (tap_z * K + tap_y) * K + tap_x
+                kernel_rows[row : row + 1, 0:C] = jnp.sum(total, axis=0, keepdims=True)
 
     for tap_z in range(K):
         kernel_layer(tap_z)
@@ -460,11 +460,13 @@
     )
 
     wait_bytes(k_in3, recv_sem.at[7])
-    k_all[sample] = add_all(k_out3[...], k_in3, NZ - 1).astype(BF16)
-    send_all(
-        x_peers, lambda peer: k_all.at[sample], lambda slot: k_all.at[sample],
-        send_sem.at[8], recv_sem.at[8],
-    )
+    k_share[...] = add_all(k_out3[...], k_in3, NZ - 1).astype(BF16)
+    k_mine = k_hbm.at[pl.ds(sample * K_SHARE, K_SHARE)]
+    send_all(
+        x_peers, lambda peer: k_share, lambda slot: k_mine, send_sem.at[8], recv_sem.at[8]
+    )
+    k_keep = pltpu.make_async_copy(k_share, k_mine, store_sem.at[2])
+    k_keep.start()
 
     wait_bytes(w_share.at[0 : (NY - 1) * PART], recv_sem.at[3])
     mine = w_hbm.at[pl.ds(sample * W_SHARE, W_SHARE)]
@@ -474,58 +476,59 @@
     )
     keep = pltpu.make_async_copy(w_share.at[0:W_SHARE], mine, store_sem.at[3])
     keep.start()
-
-    wait_bytes(k_all.at[0 : NS - 1], recv_sem.at[8])
-    rows = k_all[...].astype(F32).reshape(K_TILES * TILE, LANES)[:, 0:C] * PARAM_SCALE
-    for pair in range(K * K):
-        gkernel_ref[pair // K, pair % K] = rows[pair * K : (pair + 1) * K]
-    stores[2].start()
 
     for side in range(2):
         wait_bytes(rims.at[side], halo_send.at[side])
         wait_bytes(grims.at[side], halo_send.at[2 + side])
     sent = (
         w_in1, w_in2, w_in3, w_share.at[0 : (NY - 1) * PART], w_hbm.at[0 : (NS - 1) * W_SHARE],
-        k_in1, k_in2, k_in3, k_all.at[0 : NS - 1],
+        k_in1, k_in2, k_in3, k_hbm.at[0 : (NS - 1) * K_SHARE],
     )
     for index, ref in enumerate(sent):
         wait_bytes(ref, send_sem.at[index])
     for store in stores:
         store.wait()
     keep.wait()
+    k_keep.wait()
+    wait_bytes(k_hbm.at[0 : (NS - 1) * K_SHARE], recv_sem.at[8])
     wait_bytes(w_hbm.at[0 : (NS - 1) * W_SHARE], recv_sem.at[4])
 
 
 def write_out(
-    mixed_in, gfield_in, gkernel_in, tiles_in,
+    mixed_in, gfield_in, k_in, w_in,
     mixed_out, gfield_out, gkernel_out, gwin_out, gwout_out, gbin_out, gvec_out,
-    mixed, gfield, gkernel, gwin, gwout, gbin, gvec, tiles, sem,
+    mixed, gfield, gkernel, gwin, gwout, gbin, gvec, k_tiles, w_tiles, sem,
 ):
     def copies(pairs, first):
         return [pltpu.make_async_copy(a, b, sem.at[first + i]) for i, (a, b) in enumerate(pairs)]
 
-    load_tiles, = copies([(tiles_in, tiles)], 0)
-    loads = copies([(mixed_in, mixed), (gfield_in, gfield), (gkernel_in, gkernel)], 1)
-    passed = copies([(mixed, mixed_out), (gfield, gfield_out), (gkernel, gkernel_out)], 4)
-    made = copies([(gwin, gwin_out), (gwout, gwout_out), (gbin, gbin_out), (gvec, gvec_out)], 7)
-    load_tiles.start()
+    loads = copies([(w_in, w_tiles), (k_in, k_tiles), (mixed_in, mixed), (gfield_in, gfield)], 0)
+    stores = copies([
+        (mixed, mixed_out), (gfield, gfield_out), (gkernel, gkernel_out), (gwin, gwin_out),
+        (gwout, gwout_out), (gbin, gbin_out), (gvec, gvec_out),
+    ], 4)
     for load in loads:
         load.start()
-    load_tiles.wait()
+    loads[0].wait()
     for base, dest in ((0, gwin), (18, gwout)):
         for part in range(H // LANES):
-            block = tiles[base + 6 * part : base + 6 * part + 6].astype(F32) * PARAM_SCALE
+            block = w_tiles[base + 6 * part : base + 6 * part + 6].astype(F32) * PARAM_SCALE
             dest[:, part * LANES : (part + 1) * LANES] = block.reshape(C, LANES)
-    last = tiles[36].astype(F32) * PARAM_SCALE
+    last = w_tiles[36].astype(F32) * PARAM_SCALE
     gbin[...] = last[0:3]
     gvec[...] = last[3:7, 0:C]
-    for copy in made:
-        copy.start()
-    for load, copy in zip(loads, passed):
+    for store in stores[3:]:
+        store.start()
+    loads[1].wait()
+    rows = k_tiles[...].astype(F32).reshape(K_TILES * TILE, LANES)[:, 0:C] * PARAM_SCALE
+    for pair in range(K * K):
+        gkernel[pair // K, pair % K] = rows[pair * K : (pair + 1) * K]
+    stores[2].start()
+    for load, store in zip(loads[2:], stores):
         load.wait()
-        copy.start()
-    for copy in passed + made:
-        copy.wait()
+        store.start()
+    for store in stores:
+        store.wait()
 
 
 def local(
@@ -571,7 +574,7 @@
             (W_TILES,), (NS - 1, W_SHARE), (NY * PART,), (NY - 1, PART), (PART,), (NZ - 1, PART),
             (NY * PART,),
             (K_TILES,), (NS - 1, K_SHARE), (K_SHARE,), (NY - 1, K_SHARE), (K_SHARE,),
-            (NZ - 1, K_SHARE), (NS, K_SHARE),
+            (NZ - 1, K_SHARE), (K_SHARE,),
         )),
         *(pltpu.VMEM(shape, dtype) for shape, dtype in (
             ((E, E, E * C), BF16), ((E, E * E), jnp.int32), ((1, NY * NZ), jnp.int32),
@@ -579,7 +582,7 @@
             ((H // LANES, LANES), F32), ((C, H), BF16), ((1, C), F32), ((1, C), F32),
             ((E, E, E * C), BF16),
         )),
-        *(pltpu.VMEM(out.shape, out.dtype) for out in outs[:3]),
+        *(pltpu.VMEM(out.shape, out.dtype) for out in outs[:2]),
         pltpu.SemaphoreType.DMA((4,)),
         pltpu.SemaphoreType.DMA((4,)),
         pltpu.SemaphoreType.DMA((9,)),
@@ -590,7 +593,9 @@
     ]
     results = pl.pallas_call(
         body,
-        out_shape=outs[:3] + (jax.ShapeDtypeStruct((W_TILES, TILE, LANES), BF16),),
+        out_shape=outs[:2] + tuple(
+            jax.ShapeDtypeStruct((tiles, TILE, LANES), BF16) for tiles in (K_TILES, W_TILES)
+        ),
         in_specs=[hbm] * 12,
         out_specs=[hbm] * 4,
         scratch_shapes=scratch,
@@ -620,6 +625,7 @@
         out_specs=[hbm] * 7,
         scratch_shapes=[
             *(pltpu.VMEM(out.shape, out.dtype) for out in outs),
+            pltpu.VMEM((K_TILES, TILE, LANES), BF16),
             pltpu.VMEM((W_TILES, TILE, LANES), BF16),
             pltpu.SemaphoreType.DMA((11,)),
         ],

time: 52.7 us -> 51.8 us (0.983)
  Pallas kernels: 51.9 us -> 51 us
    pallas_call x1, Pallas kernels: 50.1 us -> 49.1 us  [local(): pl.pallas_call(body, out_shape=outs[:2] + tuple((jax.ShapeDtypeStruct((ti...]
where the time goes in v6:
time: 51.8 us; the launch traced here: 51.6 us
  Pallas kernels  51 us (98%)
  between operations  0.65 us (1%)
    pallas_call x1, Pallas kernels, local(): pl.pallas_call(body, out_shape=outs[:2] + tuple((jax.ShapeDtypeStruct((ti...  49.1 us
    pallas_call x1, Pallas kernels, local(): pl.pallas_call(write_out, out_shape=outs, in_specs=[hbm] * 4, out_specs=[...  1.83 us

profile of v6, /device:TPU:1, one launch (start us, length us, event | category | flops | bytes accessed | tf_op | source)
XLA Modules:
  0.0 51.6 jit_solution(6639819033988313399)
XLA Ops:
  0.6 49.1 %block_step.1 = (bf16[8,8,768]{2,1,0:T(8,128)(2,1)}, bf16[8,8,768]{2,1,0:T(8,128)(2,1)}, bf16[8,16,128]{2,1,0:T(8,128)(2,1)}, bf16[40,16,128]{2,1,0:T(8,128)(2,1)}) custom-call(bf16[8,8,768]{2,1,0:T(8,128)(2,1)} %bitcast.15, s32[8,64]{1,0:T(8,128)} %bitcast.20, s32[1,128]{1,0:T(1,128)} %bitcast.23, f32[5,5,5,96]{3,2,1,0:T(8,128)} %dw_hbm.1, ...), custom_call_target="tpu_custom_call" | custom-call | flops 400000000 | bytes 1500000 | tf_op jit(solution)/shard_map/block_step/pallas_call | solution.py:594
  49.8 1.8 %write_results.1 = (bf16[8,8,768]{2,1,0:T(8,128)(2,1)}, bf16[8,8,768]{2,1,0:T(8,128)(2,1)}, f32[5,5,5,96]{3,2,1,0:T(8,128)}, f32[96,384]{1,0:T(8,128)}, f32[96,3...) custom-call(bf16[8,8,768]{2,1,0:T(8,128)(2,1)} %get-tuple-element.18.mixed_in, ...), custom_call_target="tpu_custom_call" | custom-call | bytes 1000000 | tf_op jit(solution)/shard_map/write_results/pallas_call | solution.py:621
